TPU v7x, 256 devices: a whole 4x4x8 slice. The times are simulated.
256 devices in a mesh: dp: 16 (over x, z_hi, core), expert: 4 (over z_lo), mp: 4 (over y).
Axes of the slice: x: 4, y: 4, z: 8 (z_hi: 2, z_lo: 4; z = z_hi * 4 + z_lo), core: 2. Of those that a mesh axis runs over, the one named last changes fastest.
Arguments:
- hidden: bfloat16 [4, 8192, 6144], P('expert', 'dp', 'mp'), may hold values from -22 to 22
- out_grad: bfloat16 [4, 8192, 2080], P('expert', 'dp', 'mp'), may hold values from -1 to 1
- master: float32 [4, 6144, 2080], P('expert', ('mp', 'dp')), may hold values from -6 to 6
- row_prev: float32 [4, 6144], P('expert', ('mp', 'dp')), may hold values from 0.03 to 0.3
- col_prev: float32 [4, 2080], P('expert'), may hold values from 0.03 to 0.3
Outputs:
- params: bfloat16 [4, 6144, 2080], P('expert', 'mp')
- master_new: float32 [4, 6144, 2080], P('expert', ('mp', 'dp'))
- direction: float32 [4, 6144, 2080], P('expert', ('mp', 'dp'))
- row_stat: float32 [4, 6144], P('expert', ('mp', 'dp'))
- col_stat: float32 [4, 2080], P('expert')
All inputs are finite; a program needn't handle non-finite values.
Results may differ from a plain program's by a relative error of at most 0.0004.
Values may be sent and summed in bfloat16 or wider, within the bound.
A program may use at most 128 MiB of HBM per device.

v0:
```python
import jax
import jax.numpy as jnp
from jax import lax
from jax.sharding import PartitionSpec as P

D = 2080
FF = 6144
STEP = 100


DECAY_POWER = 0.8
EPS_GRAD = 1e-30
LEARNING_RATE = 0.01
CONTRACT_TOKENS = (((0,), (0,)), ((), ()))


def factored_step(gradient, row_old, col_old, first_sum):
    decay_rate = 1.0 - STEP ** (-DECAY_POWER)
    plain_squares = gradient * gradient
    squares = plain_squares + EPS_GRAD
    row_stat = decay_rate * row_old + (1.0 - decay_rate) * jnp.mean(squares, axis=1)
    col_part = jnp.sum(squares, axis=0)
    col_sum = first_sum(col_part)
    col_stat = decay_rate * col_old + (1.0 - decay_rate) * (col_sum / FF)
    scaled = gradient / jnp.sqrt(row_stat[:, None] * col_stat[None, :])
    total_squares = lax.psum(jnp.sum(scaled * scaled), ("dp", "mp"))
    update_rms = jnp.sqrt(total_squares / (FF * D))
    direction = scaled / jnp.maximum(1.0, update_rms)
    return (direction, row_stat, col_stat)


def local(hidden, out_grad, master, row_prev, col_prev):
    features = lax.all_gather(out_grad[0], "mp", axis=1, tiled=True)
    local_hidden = hidden[0]
    gradient = lax.psum_scatter(
        lax.dot_general(
            local_hidden, features, CONTRACT_TOKENS, preferred_element_type=jnp.float32
        ),
        "dp",
        scatter_dimension=0,
        tiled=True,
    )

    def joint_stats(stat_values):
        return lax.psum(stat_values, ("dp", "mp"))

    direction, row_stat, col_stat = factored_step(gradient, row_prev[0], col_prev[0], joint_stats)
    master_new = master[0] - LEARNING_RATE * direction
    new_params = lax.all_gather(master_new.astype(jnp.bfloat16), "dp", axis=0, tiled=True)
    results = [(new_params, master_new, direction, row_stat, col_stat)]
    return tuple((jnp.stack([result[position] for result in results]) for position in range(5)))


def solution(mesh):
    in_specs = (
        P("expert", "dp", "mp"),
        P("expert", "dp", "mp"),
        P("expert", ("mp", "dp"), None),
        P("expert", ("mp", "dp")),
        P("expert", None),
    )
    out_specs = (
        P("expert", "mp", None),
        P("expert", ("mp", "dp"), None),
        P("expert", ("mp", "dp"), None),
        P("expert", ("mp", "dp")),
        P("expert", None),
    )
    return jax.shard_map(local, mesh=mesh, in_specs=in_specs, out_specs=out_specs, check_vma=False)
```

profile of v0, /device:TPU:1, one launch (start us, length us, event | category | flops | bytes accessed | tf_op | source)
XLA Modules:
  0.0 952.1 jit_solution(11516915283859080865)
XLA Ops:
  7.2 0.0 copy-start
  7.2 0.0 all-gather.6.cloned.1.call-start
  7.2 0.7 all-gather.6.cloned.1.call-update
  7.9 0.0 reduce-scatter.2.cloned.1.call-start
  8.0 39.4 %all-gather.6.cloned.1.call-done = bf16[1,512,2080]{1,2,0:T(8,128)(2,1)} async-done(((bf16[1,512,520]{1,2,0:T(8,128)(2,1)}), bf16[1,512,2080]{1,2,0:T(8,128)(2,1)}) %all-gather.6.cloned.1.call-update) | async-done | bytes 2129936 | tf_op jit(solution)/shard_map/all_gather | solution.py:33
  47.3 0.0 copy-done
  47.3 8.5 fusion
  55.8 0.0 copy-start.3
  55.9 0.0 copy-start.4
  55.9 0.0 reduce-scatter.2.cloned.1.call-update
  55.9 0.0 copy-start.2
  55.9 0.0 all-gather.4.cloned.1.call-start
  55.9 0.6 copy-done.3
  56.6 177.8 %reduce-scatter.2.cloned.1.call-done = f32[96,2080]{1,0:T(8,128)} async-done(((f32[1536,2080]{1,0:T(8,128)}), f32[96,2080]{1,0:T(8,128)}) %reduce-scatter.2.cloned.1.call-update) | async-done | bytes 798736 | tf_op jit(solution)/shard_map/reduce_scatter | solution.py:35
  234.4 0.0 copy-start.1
  234.4 1.5 fusion.4
  235.9 389.3 %psum.14 = f32[2080]{0:T(1024)S(1)} all-reduce(f32[2080]{0:T(1024)S(1)} %get-tuple-element.11), channel_id=1, replica_groups=mesh['dp'=16,'expert'=4,'mp'=4] {'dp','mp'}, use_global_device_ids=true, to_apply=%region_3.0 | all-reduce | flops 2080 | bytes 16640 | tf_op jit(solution)/shard_map/psum | solution.py:45
  625.2 0.0 copy-done.4
  625.2 2.0 multiply_reduce_fusion
  627.2 201.6 %psum.15 = f32[]{:T(128)} all-reduce(f32[]{:T(128)} %multiply_reduce_fusion), channel_id=1, replica_groups=mesh['dp'=16,'expert'=4,'mp'=4] {'dp','mp'}, use_global_device_ids=true, to_apply=%region_5.0 | all-reduce | flops 1 | bytes 8 | tf_op jit(solution)/shard_map/psum | solution.py:26
  829.5 0.0 copy-done.2
  829.5 0.0 copy-done.1
  829.5 1.6 fusion.6
  831.1 0.0 all-gather.4.cloned.1.call-update
  831.1 0.6 broadcast_in_dim.4
  831.7 0.5 bitcast_add_fusion
  832.2 103.8 %all-gather.4.cloned.1.call-done = bf16[1536,2080]{1,0:T(8,128)(2,1)} async-done(((bf16[96,2080]{1,0:T(8,128)(2,1)}), bf16[1536,2080]{1,0:T(8,128)(2,1)}) %all-gather.4.cloned.1.call-update) | async-done | bytes 6389776 | tf_op jit(solution)/shard_map/all_gather | solution.py:49
  936.0 9.6 %copy.10 = bf16[1,1536,2080]{1,2,0:T(8,128)(2,1)} copy(bf16[1,1536,2080]{2,1,0:T(8,128)(2,1)} %bitcast.21) | data formatting | bytes 12779520
  (3 shorter events, 0.0 us)
Async XLA Ops:
  7.2 40.2 %copy-start = (bf16[1,512,1536]{2,1,0:T(8,128)(2,1)S(1)}, bf16[1,512,1536]{2,1,0:T(8,128)(2,1)}, u32[]{:S(2)}) copy-start(bf16[1,512,1536]{2,1,0:T(8,128)(2,1)} %param.5) | copy-start | bytes 4718596
  7.2 40.2 %all-gather.6.cloned.1.call-start = ((), (), s32[]{:S(2)}) async-start(), calls=%async_computation.3 | async-start | bytes 2662400 | tf_op jit(solution)/shard_map/all_gather | solution.py:33
  7.9 226.5 %reduce-scatter.2.cloned.1.call-start = ((), (), s32[]{:S(2)}) async-start(), calls=%async_computation.1 | async-start | bytes 14204928 | tf_op jit(solution)/shard_map/reduce_scatter | solution.py:35
  55.8 0.7 copy-start.3
  55.9 569.3 %copy-start.4 = (f32[1,96]{1,0:T(1,128)S(1)}, f32[1,96]{1,0:T(1,128)}, u32[]{:S(2)}) copy-start(f32[1,96]{1,0:T(1,128)} %param.8) | copy-start | bytes 1156
  55.9 773.6 %copy-start.2 = (f32[1,96,2080]{2,1,0:T(8,128)S(1)}, f32[1,96,2080]{2,1,0:T(8,128)}, u32[]{:S(2)}) copy-start(f32[1,96,2080]{2,1,0:T(8,128)} %param.7) | copy-start | bytes 2396164
  55.9 880.1 %all-gather.4.cloned.1.call-start = ((), (), s32[]{:S(2)}) async-start(), calls=%async_computation.2 | async-start | bytes 7102464 | tf_op jit(solution)/shard_map/all_gather | solution.py:49
  234.4 595.1 %copy-start.1 = (f32[96,2080]{1,0:T(8,128)S(1)}, f32[96,2080]{1,0:T(8,128)}, u32[]{:S(2)}) copy-start(f32[96,2080]{1,0:T(8,128)} %reduce-scatter.2.cloned.1.call-done) | copy-start | bytes 2396164
Sparse Core Ops, SparseCore 0:
  9.8 37.4 all-gather.5
  56.0 178.3 reduce-scatter.1
  831.2 104.7 all-gather.3
where the time goes:
time: 953 us; the launch traced here: 952 us
  blocking collectives  591 us (62%)
  waiting for transfers between devices  322 us (34%)
  between operations  14.5 us (2%)
  local copies, waits for them, and re-layouts  10.9 us (1%)
    psum x1, blocking collectives, joint_stats(): return lax.psum(stat_values, ('dp', 'mp'))  389 us
    psum x1, blocking collectives, factored_step(): total_squares = lax.psum(jnp.sum(scaled * scaled), ('dp', 'mp'))  202 us
    reduce_scatter x1, waiting for transfers between devices, local(): lax.psum_scatter(lax.dot_general(local_hidden, features, CONTRACT_TOKENS,...  178 us
    all_gather x1, waiting for transfers between devices, local(): lax.all_gather(master_new.astype(jnp.bfloat16), 'dp', axis=0, tiled=True)  104 us
    all_gather x1, waiting for transfers between devices, local(): features = lax.all_gather(out_grad[0], 'mp', axis=1, tiled=True)  39.4 us
  transfers between devices with their start and end apart: 3, of which 3 were waited for; matrix products, arithmetic and copies ran while one was open for 0% of the time, Pallas kernels for 0%

commit v1 on v0

v1 whole, which is shorter than its diff:
```python
import functools

import jax
import jax.numpy as jnp
from jax import lax
from jax.experimental import pallas as pl
from jax.experimental.pallas import tpu as pltpu
from jax.sharding import PartitionSpec as P

D = 2080
FF = 6144
STEP = 100
DECAY_POWER = 0.8
EPS_GRAD = 1e-30
LEARNING_RATE = 0.01

NX, NH, NC, NY = 4, 2, 2, 4
TOK = 512
ROWS = 96
SLOTS = NX * NH
WIDE = 512
BLOCK = D // NY
REST = BLOCK - WIDE
TAIL = 128
NB = NY + 1
PIECES = 3
PIECE = ROWS // PIECES
MESH = pl.DeviceIdType.MESH
F32 = jnp.float32
BF16 = jnp.bfloat16


def kernel(hidden_ref, grad_ref, master_ref, row_ref, col_ref,
           params_ref, new_ref, dir_ref, row_out, col_out,
           hid, turned, lhs, feats, tailf, wide_p, tail_p,
           got_a, got_b, got_c, got_z, tgot_a, tgot_b, tgot_c, tgot_z,
           gsum, tsum, nat, stat_a, stat_b, full,
           load_sem, copy_sem,
           ysend, yrecv, csend, crecv, hsend, hrecv,
           xsend, xrecv, zsend, zrecv, ssend, srecv,
           gsend, grecv, out_sem):
    dp, ex, y = lax.axis_index("dp"), lax.axis_index("expert"), lax.axis_index("mp")
    x, h, c = dp // 4, lax.rem(dp // 2, 2), lax.rem(dp, 2)
    step = 1 - 2 * c

    def dev(dx=0, dh=0, dc=0, dy=0):
        return (
            (lax.rem(x + dx + NX, NX) * NH + lax.rem(h + dh, NH)) * NC + lax.rem(c + dc, NC),
            ex,
            lax.rem(y + dy + NY, NY),
        )

    def remote(src, dst, send, recv, to):
        copy = pltpu.make_async_remote_copy(
            src_ref=src, dst_ref=dst, send_sem=send, recv_sem=recv,
            device_id=to, device_id_type=MESH)
        copy.start()
        return copy

    started = []

    load_h = pltpu.make_async_copy(hidden_ref, hid, load_sem.at[0])
    load_h.start()
    mine = pl.ds(pl.multiple_of(c * TOK, TOK), TOK)
    other = pl.ds(pl.multiple_of((1 - c) * TOK, TOK), TOK)
    load_g = pltpu.make_async_copy(grad_ref, feats.at[y, mine], load_sem.at[1])
    load_g.start()

    group_a = [(dx, dc) for dx in range(NX) for dc in range(NC) if (dx, dc) != (0, 0)]
    group_b = [(dy, dh) for dy in range(NY) for dh in range(NH) if (dy, dh) != (0, 0)]
    barrier = pltpu.get_barrier_semaphore()
    for dx, dc in group_a:
        pl.semaphore_signal(barrier, 1, device_id=dev(dx=dx, dc=dc), device_id_type=MESH)
    for dy, dh in group_b:
        pl.semaphore_signal(barrier, 1, device_id=dev(dy=dy, dh=dh), device_id_type=MESH)
    pl.semaphore_wait(barrier, len(group_a) + len(group_b))

    load_g.wait()
    own = feats.at[y, mine]
    up = remote(own, own, ysend.at[0], yrecv.at[2], dev(dy=1))
    down = remote(own, own, ysend.at[1], yrecv.at[1], dev(dy=-1))
    sib = remote(own, own, csend.at[0], crecv.at[0], dev(dc=1))
    started += [up, down, sib]

    load_h.wait()
    for g in range(4):
        part = hid[:, pl.ds(384 * g, 384)].T
        for q in range(4):
            turned[2 * g + q // 2, q % 2] = part[ROWS * q:ROWS * (q + 1), :]
    give = remote(turned.at[:, 1 - c], lhs.at[:, :, mine], hsend, hrecv, dev(dc=1))
    keep = pltpu.make_async_copy(turned.at[:, c], lhs.at[:, :, mine], copy_sem)
    keep.start()
    keep.wait()
    give.wait()

    wides = [wide_p.at[t] for t in range(NY)] + [tail_p]
    as_ = [got_a.at[t] for t in range(NY)] + [tgot_a]
    bs_ = [got_b.at[t] for t in range(NY)] + [tgot_b]
    cs_ = [got_c.at[t] for t in range(NY)] + [tgot_c]
    zs_ = [got_z.at[t] for t in range(NY)] + [tgot_z]
    offs = (0, 1, 3, 2)

    def chunk(t, dx):
        return wides[t].at[pl.ds(2 * lax.rem(x + dx + NX, NX), 2)]

    def product(t):
        left = lhs[...].reshape(SLOTS * ROWS, 2 * TOK)
        if t < NY:
            b = lax.rem(y + offs[t], NY)

            @pl.loop(0, WIDE // 256)
            def _(n):
                cols = pl.ds(pl.multiple_of(n * 256, 256), 256)
                wide_p[t, :, :, cols] = jnp.dot(
                    left, feats[b, :, cols], preferred_element_type=F32
                ).reshape(SLOTS, ROWS, 256)
        else:
            tail_p[...] = jnp.dot(
                left, tailf[...], preferred_element_type=F32
            ).reshape(SLOTS, ROWS, TAIL)
        started.append(remote(chunk(t, 2), as_[t], xsend.at[0, t], xrecv.at[0, t], dev(dx=step)))
        started.append(remote(chunk(t, -step), bs_[t], xsend.at[1, t], xrecv.at[1, t], dev(dx=-step)))

    def recv(dst, sem):
        pltpu.make_async_remote_copy(
            src_ref=dst, dst_ref=dst, send_sem=sem, recv_sem=sem,
            device_id=dev(dc=1), device_id_type=MESH).wait_recv()

    def forward_sum(t):
        recv(as_[t], xrecv.at[0, t])
        ref = chunk(t, step)
        ref[...] = ref[...] + as_[t][...]
        started.append(remote(ref, cs_[t], xsend.at[2, t], xrecv.at[2, t], dev(dx=step)))

    def own_sum(t):
        recv(bs_[t], xrecv.at[1, t])
        recv(cs_[t], xrecv.at[2, t])
        ref = chunk(t, 0)
        ref[...] = ref[...] + bs_[t][...] + cs_[t][...]
        started.append(remote(ref.at[1 - h], zs_[t], zsend.at[t], zrecv.at[t], dev(dh=1)))

    def finish(t):
        recv(zs_[t], zrecv.at[t])
        total = chunk(t, 0).at[h][...] + zs_[t][...]
        if t < NY:
            gsum[lax.rem(y + offs[t], NY)] = total
        else:
            tsum[...] = total

    def sib_forward(t):
        b = lax.rem(y + offs[t], NY)
        started.append(remote(feats.at[b, mine], feats.at[b, mine],
                              csend.at[t], crecv.at[t], dev(dc=1)))

    def block(t):
        b = lax.rem(y + offs[t], NY)
        return feats.at[b, mine], feats.at[b, other]

    recv(block(0)[1], crecv.at[0])
    product(0)
    forward_sum(0)
    recv(block(1)[0], yrecv.at[1])
    recv(block(2)[0], yrecv.at[2])
    on = feats.at[lax.rem(y - step + NY, NY), mine]
    started.append(remote(on, on, ysend.at[2], yrecv.at[3], dev(dy=step)))
    sib_forward(1)
    sib_forward(2)
    recv(block(1)[1], crecv.at[1])
    product(1)
    recv(block(2)[1], crecv.at[2])
    product(2)
    own_sum(0)
    forward_sum(1)
    recv(block(3)[0], yrecv.at[3])
    sib_forward(3)
    forward_sum(2)
    recv(block(3)[1], crecv.at[3])
    product(3)
    tailf[...] = jnp.zeros_like(tailf)
    for b in range(NY):
        tailf[:, REST * b:REST * (b + 1)] = feats[b, :, WIDE:BLOCK]
    product(4)
    own_sum(1)
    finish(0)
    forward_sum(3)
    forward_sum(4)
    own_sum(2)
    finish(1)
    own_sum(3)
    own_sum(4)
    finish(2)
    finish(3)
    finish(4)

    decay = 1.0 - STEP ** (-DECAY_POWER)
    for b in range(NY):
        nat[:, BLOCK * b:BLOCK * b + WIDE] = gsum[b]
        nat[:, BLOCK * b + WIDE:BLOCK * (b + 1)] = tsum[:, REST * b:REST * (b + 1)]
    squares = nat[...] * nat[...]
    row_mean = jnp.sum(squares + EPS_GRAD, axis=1, keepdims=True) / D
    eye = (lax.broadcasted_iota(jnp.int32, (ROWS, ROWS), 0)
           == lax.broadcasted_iota(jnp.int32, (ROWS, ROWS), 1))
    row_old = jnp.sum(jnp.where(eye, row_ref[...], 0.0), axis=1, keepdims=True)
    row_stat = decay * row_old + (1.0 - decay) * row_mean
    row_out[...] = jnp.sum(jnp.where(eye, row_stat, 0.0), axis=0, keepdims=True)
    slot_a = x * NC + c
    slot_b = y * NH + h
    stat_a[slot_a, 0:1] = jnp.sum(squares + EPS_GRAD, axis=0, keepdims=True)
    stat_a[slot_a, 1:2] = jnp.sum(squares / row_stat, axis=0, keepdims=True)
    for i, (dx, dc) in enumerate(group_a):
        started.append(remote(stat_a.at[slot_a], stat_a.at[slot_a], ssend.at[0, i], srecv.at[0, i],
                              dev(dx=dx, dc=dc)))
    for i, (dx, dc) in enumerate(group_a):
        recv(stat_a.at[lax.rem(x - dx + NX, NX) * NC + lax.rem(c + dc, NC)], srecv.at[0, i])
    stat_b[slot_b] = jnp.sum(stat_a[...], axis=0)
    for i, (dy, dh) in enumerate(group_b):
        started.append(remote(stat_b.at[slot_b], stat_b.at[slot_b], ssend.at[1, i], srecv.at[1, i],
                              dev(dy=dy, dh=dh)))
    for i, (dy, dh) in enumerate(group_b):
        recv(stat_b.at[lax.rem(y - dy + NY, NY) * NH + lax.rem(h + dh, NH)], srecv.at[1, i])
    sums = jnp.sum(stat_b[...], axis=0)
    col_stat = decay * col_ref[...] + (1.0 - decay) * (sums[0:1] / FF)
    col_out[...] = col_stat
    update_rms = jnp.sqrt(jnp.sum(sums[1:2] / col_stat, axis=1, keepdims=True) / (FF * D))
    scale = 1.0 / jnp.maximum(1.0, update_rms)
    direction = nat[...] * lax.rsqrt(row_stat) * (lax.rsqrt(col_stat) * scale)
    dir_ref[...] = direction
    master_new = master_ref[...] - LEARNING_RATE * direction
    new_ref[...] = master_new
    slot = x * NH + h
    full[slot, c] = master_new.astype(BF16)

    def piece(dx, dh, core, p):
        return full.at[lax.rem(x + dx + NX, NX) * NH + lax.rem(h + dh, NH), core, pl.ds(PIECE * p, PIECE)]

    outs = []

    def ready(ref_of, share, n):
        ref = ref_of
        if share is not None:
            started.append(remote(ref, ref, gsend.at[share], grecv.at[share], dev(dc=1)))
        del n

    def sem(kind, p):
        return kind * PIECES + p

    def send_along(kind, dh, dx, p, src_dx=0):
        ref = piece(src_dx, dh, c, p)
        started.append(remote(ref, ref, gsend.at[sem(kind, p)], grecv.at[sem(kind, p)], dev(dx=dx)))

    def share(kind, dx, dh, p):
        ref = piece(dx, dh, c, p)
        started.append(remote(ref, ref, gsend.at[sem(kind, p)], grecv.at[sem(kind, p)], dev(dc=1)))

    def got(kind, dx, dh, p, core):
        recv(piece(dx, dh, core, p), grecv.at[sem(kind, p)])

    for p in range(PIECES):
        ref = piece(0, 0, c, p)
        started.append(remote(ref, ref, gsend.at[sem(0, p)], grecv.at[sem(0, p)], dev(dh=1)))
        send_along(1, 0, 1, p)
        send_along(3, 0, -1, p)
    for p in range(PIECES):
        share(7, 0, 0, p)

    def pass_on(dh, p):
        kinds = (1, 3) if dh == 0 else (2, 4)
        got(kinds[0], -1, dh, p, c)
        got(kinds[1], 1, dh, p, c)
        send_along(5 + dh, dh, step, p, src_dx=-step)
        share(9 + dh, 1, dh, p)
        share(11 + dh, -1, dh, p)

    for p in range(PIECES):
        got(0, 0, 1, p, c)
        send_along(2, 1, 1, p)
        send_along(4, 1, -1, p)
        share(8, 0, 1, p)
        pass_on(0, p)
    for p in range(PIECES):
        pass_on(1, p)
        got(5, 2, 0, p, c)
        share(13, 2, 0, p)
    for p in range(PIECES):
        got(6, 2, 1, p, c)
        share(14, 2, 1, p)
    for p in range(PIECES):
        for dx in range(NX):
            pass
    for p in range(PIECES):
        got(7, 0, 0, p, 1 - c)
        got(8, 0, 1, p, 1 - c)
        for dh in range(NH):
            got(9 + dh, 1, dh, p, 1 - c)
            got(11 + dh, -1, dh, p, 1 - c)
            got(13 + dh, 2, dh, p, 1 - c)
    out = pltpu.make_async_copy(full, params_ref, out_sem)
    out.start()
    out.wait()
    for copy in started:
        copy.wait_send()


def local(hidden, out_grad, master, row_prev, col_prev):
    vmem = pl.BlockSpec(memory_space=pltpu.VMEM)
    anywhere = pl.BlockSpec(memory_space=pl.ANY)
    dma = pltpu.SemaphoreType.DMA
    params, master_new, direction, row_stat, col_stat = pl.pallas_call(
        kernel,
        out_shape=(
            jax.ShapeDtypeStruct((SLOTS, NC, ROWS, D), BF16),
            jax.ShapeDtypeStruct((ROWS, D), F32),
            jax.ShapeDtypeStruct((ROWS, D), F32),
            jax.ShapeDtypeStruct((1, ROWS), F32),
            jax.ShapeDtypeStruct((1, D), F32),
        ),
        in_specs=[anywhere, anywhere, vmem, vmem, vmem],
        out_specs=(anywhere, vmem, vmem, vmem, vmem),
        scratch_shapes=[
            pltpu.VMEM((TOK, NC * SLOTS * ROWS), BF16),
            pltpu.VMEM((SLOTS, NC, ROWS, TOK), BF16),
            pltpu.VMEM((SLOTS, ROWS, NC * TOK), BF16),
            pltpu.VMEM((NY, NC * TOK, BLOCK), BF16),
            pltpu.VMEM((NC * TOK, TAIL), BF16),
            pltpu.VMEM((NY, SLOTS, ROWS, WIDE), F32),
            pltpu.VMEM((SLOTS, ROWS, TAIL), F32),
            pltpu.VMEM((NY, NH, ROWS, WIDE), F32),
            pltpu.VMEM((NY, NH, ROWS, WIDE), F32),
            pltpu.VMEM((NY, NH, ROWS, WIDE), F32),
            pltpu.VMEM((NY, ROWS, WIDE), F32),
            pltpu.VMEM((NH, ROWS, TAIL), F32),
            pltpu.VMEM((NH, ROWS, TAIL), F32),
            pltpu.VMEM((NH, ROWS, TAIL), F32),
            pltpu.VMEM((ROWS, TAIL), F32),
            pltpu.VMEM((NY, ROWS, WIDE), F32),
            pltpu.VMEM((ROWS, TAIL), F32),
            pltpu.VMEM((ROWS, D), F32),
            pltpu.VMEM((NX * NC, 2, D), F32),
            pltpu.VMEM((NY * NH, 2, D), F32),
            pltpu.VMEM((SLOTS, NC, ROWS, D), BF16),
            dma((2,)), dma,
            dma((3,)), dma((4,)), dma((4,)), dma((4,)), dma, dma,
            dma((3, NB)), dma((3, NB)), dma((NB,)), dma((NB,)), dma((2, 7)), dma((2, 7)),
            dma((15 * PIECES,)), dma((15 * PIECES,)), dma,
        ],
        compiler_params=pltpu.CompilerParams(
            collective_id=0, has_side_effects=True, vmem_limit_bytes=60 * 2**20),
        cost_estimate=pl.CostEstimate(
            flops=2 * TOK * FF // NY * D, bytes_accessed=16 * 2**20, transcendentals=0),
        name="factored_step",
    )(hidden[0], out_grad[0], master[0], row_prev, col_prev)
    return (params.reshape(1, SLOTS * NC * ROWS, D), master_new[None], direction[None],
            row_stat, col_stat)


def solution(mesh):
    in_specs = (
        P("expert", "dp", "mp"),
        P("expert", "dp", "mp"),
        P("expert", ("mp", "dp"), None),
        P("expert", ("mp", "dp")),
        P("expert", None),
    )
    out_specs = (
        P("expert", "mp", None),
        P("expert", ("mp", "dp"), None),
        P("expert", ("mp", "dp"), None),
        P("expert", ("mp", "dp")),
        P("expert", None),
    )
    return jax.shard_map(local, mesh=mesh, in_specs=in_specs, out_specs=out_specs, check_vma=False)
```

time: 953 us -> 157 us (0.16)
  the two profiles are of different devices: /device:TPU:1 before, /device:TPU:33 now
where the time goes in v1:
time: 157 us; the launch traced here: 156 us
  Pallas kernels  141 us (90%)
  local copies, waits for them, and re-layouts  14.8 us (9%)
    pallas_call x1, Pallas kernels, local(): pl.pallas_call(kernel, out_shape=(jax.ShapeDtypeStruct((SLOTS, NC, ROWS,...  141 us
    unnamed x14, local copies, waits for them, and re-layouts  14.8 us

profile of v1, /device:TPU:33, one launch (start us, length us, event | category | flops | bytes accessed | tf_op | source)
XLA Modules:
  0.0 156.5 jit_solution(6164072294490204962)
XLA Ops:
  0.6 2.1 %copy.10 = bf16[1,512,520]{2,1,0:T(8,128)(2,1)} copy(bf16[1,512,520]{1,2,0:T(8,128)(2,1)} %param.6) | data formatting | bytes 1064960 | tf_op args[1]
  2.8 141.0 %factored_step.1 = (bf16[8,2,96,2080]{3,2,1,0:T(8,128)(2,1)}, f32[96,2080]{1,0:T(8,128)}, f32[96,2080]{1,0:T(8,128)}, f32[1,96]{1,0:T(1,128)}, f32[1,2080]{1,0:T(1,128)}) custom-call(bf16[512,1536]{1,0:T(8,128)(2,1)} %bitcast.10, bf16[512,520]{1,0:T(8,128)(2,1)} %bitcast.9, f32[96,2080]{1,0:T(8,128)} %bitcast.11, f32[1,96]{1,0:T(1,128)} %row_ref.1, ...), custom_call_target="tpu_custom_call" | custom-call | flops 3271557120 | bytes 16777216 | tf_op jit(solution)/shard_map/factored_step/pallas_call | solution.py:308
  143.7 0.0 copy-start.1
  143.8 0.0 copy-start
  143.8 0.0 copy-start.3
  143.8 0.0 copy-start.2
  143.8 9.8 %copy.11 = bf16[1,1536,2080]{1,2,0:T(8,128)(2,1)} copy(bf16[1,1536,2080]{2,1,0:T(8,128)(2,1)} %bitcast.6) | data formatting | bytes 12779520
  153.6 0.0 copy-done.1
  153.6 0.9 copy.16
  154.5 0.0 copy-done
  154.5 0.9 copy.17
  155.4 0.0 copy-done.3
  155.4 0.5 copy.18
  155.9 0.0 copy-done.2
  155.9 0.6 copy.19
Async XLA Ops:
  143.7 9.8 %copy-start.1 = (f32[96,2080]{1,0:T(8,128)S(1)}, f32[96,2080]{1,0:T(8,128)}, u32[]{:S(2)}) copy-start(f32[96,2080]{1,0:T(8,128)} %get-tuple-element.11) | copy-start | bytes 2396164
  143.8 10.7 %copy-start = (f32[96,2080]{1,0:T(8,128)S(1)}, f32[96,2080]{1,0:T(8,128)}, u32[]{:S(2)}) copy-start(f32[96,2080]{1,0:T(8,128)} %get-tuple-element.12) | copy-start | bytes 2396164
  143.8 11.6 %copy-start.3 = (f32[1,96]{1,0:T(1,128)S(1)}, f32[1,96]{1,0:T(1,128)}, u32[]{:S(2)}) copy-start(f32[1,96]{1,0:T(1,128)} %get-tuple-element.28) | copy-start | bytes 1156
  143.8 12.1 %copy-start.2 = (f32[1,2080]{1,0:T(1,128)S(1)}, f32[1,2080]{1,0:T(1,128)}, u32[]{:S(2)}) copy-start(f32[1,2080]{1,0:T(1,128)} %get-tuple-element.29) | copy-start | bytes 24964

commit v2 on v1

v2 whole, which is shorter than its diff:
```python
import functools

import jax
import jax.numpy as jnp
from jax import lax
from jax.experimental import pallas as pl
from jax.experimental.pallas import tpu as pltpu
from jax.sharding import PartitionSpec as P

D = 2080
FF = 6144
STEP = 100
DECAY_POWER = 0.8
EPS_GRAD = 1e-30
LEARNING_RATE = 0.01

NX, NH, NC, NY = 4, 2, 2, 4
TOK = 512
ROWS = 96
SLOTS = NX * NH
WIDE = 512
BLOCK = D // NY
REST = BLOCK - WIDE
HELD = WIDE + 16
TAIL = 128
NB = NY + 1
HALF = 1024
PART = 256
EXTRA = 128
PARTS = 5
MESH = pl.DeviceIdType.MESH
F32 = jnp.float32
BF16 = jnp.bfloat16

LEVELS = 21
REACH = 10.4 * 256
TINY = 1e-30


def split(value):
    high = value.astype(BF16)
    wide = high.astype(F32)
    inverse = pl.reciprocal(jnp.maximum(jnp.abs(wide), TINY), approx=True)
    return high, jnp.round((value - wide) * (inverse * REACH))


def encode(first, second, planes, rows):
    high_1, step_1 = split(first)
    high_2, step_2 = split(second)
    planes[0, rows] = high_1
    planes[1, rows] = high_2
    planes[2, rows] = (step_1 * LEVELS + step_2).astype(BF16)


def decode(planes, rows):
    low = planes[2, rows].astype(F32)
    step_1 = jnp.round(low * (1.0 / LEVELS))
    step_2 = low - LEVELS * step_1
    wide_1 = planes[0, rows].astype(F32)
    wide_2 = planes[1, rows].astype(F32)
    return (wide_1 + jnp.abs(wide_1) * (step_1 * (1.0 / REACH)),
            wide_2 + jnp.abs(wide_2) * (step_2 * (1.0 / REACH)))


def by_rows(count, body):
    @pl.loop(0, count // 16)
    def _(i):
        body(pl.multiple_of(i * 16, 16))


def kernel(hidden_ref, grad_ref, master_ref, row_ref, col_ref,
           params_ref, new_ref, dir_ref, row_out, col_out,
           hid, own_grad, turned, lhs, feats, tailf, wide_p, tail_p,
           out_x, out_z, tout_x, tout_z,
           got_x, got_z, tgot_x, tgot_z,
           gsum, tsum, nat, held_m, stat_a, stat_b, plain, rows_in,
           load_sem, copy_sem,
           ysend, yrecv, csend, crecv, hsend, hrecv,
           xsend, xrecv, zsend, zrecv, ssend, srecv,
           gsend, grecv):
    dp, ex, y = lax.axis_index("dp"), lax.axis_index("expert"), lax.axis_index("mp")
    x, h, c = dp // 4, lax.rem(dp // 2, 2), lax.rem(dp, 2)
    step = 1 - 2 * c

    def dev(dx=0, dh=0, dc=0, dy=0):
        return (
            (lax.rem(x + dx + NX, NX) * NH + lax.rem(h + dh, NH)) * NC + lax.rem(c + dc, NC),
            ex,
            lax.rem(y + dy + NY, NY),
        )

    def remote(src, dst, send, recv, to):
        copy = pltpu.make_async_remote_copy(
            src_ref=src, dst_ref=dst, send_sem=send, recv_sem=recv,
            device_id=to, device_id_type=MESH)
        copy.start()
        return copy

    started = []

    load_h = pltpu.make_async_copy(hidden_ref, hid, load_sem.at[0])
    load_h.start()
    mine = pl.ds(pl.multiple_of(c * TOK, TOK), TOK)
    other = pl.ds(pl.multiple_of((1 - c) * TOK, TOK), TOK)
    load_g = pltpu.make_async_copy(grad_ref, own_grad, load_sem.at[1])
    load_g.start()
    load_m = pltpu.make_async_copy(master_ref, held_m, load_sem.at[2])
    load_m.start()

    group_a = [(dx, dc) for dx in range(NX) for dc in range(NC) if (dx, dc) != (0, 0)]
    group_b = [(dy, dh) for dy in range(NY) for dh in range(NH) if (dy, dh) != (0, 0)]
    barrier = pltpu.get_barrier_semaphore()
    for dx, dc in group_a:
        pl.semaphore_signal(barrier, 1, device_id=dev(dx=dx, dc=dc), device_id_type=MESH)
    for dy, dh in group_b:
        pl.semaphore_signal(barrier, 1, device_id=dev(dy=dy, dh=dh), device_id_type=MESH)
    pl.semaphore_wait(barrier, len(group_a) + len(group_b))

    load_g.wait()
    feats[y, 0:WIDE, mine] = own_grad[0:WIDE, :]
    feats[y, WIDE:HELD, mine] = jnp.concatenate(
        [own_grad[WIDE:BLOCK, :], jnp.zeros((HELD - BLOCK, TOK), BF16)], axis=0)
    own = feats.at[y, :, mine]
    up = remote(own, own, ysend.at[0], yrecv.at[2], dev(dy=1))
    down = remote(own, own, ysend.at[1], yrecv.at[1], dev(dy=-1))
    sib = remote(own, own, csend.at[0], crecv.at[0], dev(dc=1))
    started += [up, down, sib]

    load_h.wait()
    for g in range(4):
        part = hid[:, pl.ds(384 * g, 384)].T
        for q in range(4):
            turned[2 * g + q // 2, q % 2] = part[ROWS * q:ROWS * (q + 1), :]
    give = remote(turned.at[:, 1 - c], lhs.at[:, :, mine], hsend.at[0], hrecv.at[0], dev(dc=1))
    keep = pltpu.make_async_copy(turned.at[:, c], lhs.at[:, :, mine], copy_sem)
    keep.start()
    keep.wait()
    give.wait()

    wides = [wide_p.at[t] for t in range(NY)] + [tail_p]
    offs = (0, 1, 3, 2)

    def sent_x(kind, t):
        return out_x.at[kind, t] if t < NY else tout_x.at[kind]

    def arrived_x(kind, t):
        return got_x.at[kind, t] if t < NY else tgot_x.at[kind]

    def chunk(t, dx):
        return wides[t].at[pl.ds(2 * lax.rem(x + dx + NX, NX), 2)]

    def send_x(kind, t, dx):
        started.append(remote(sent_x(kind, t), arrived_x(kind, t),
                              xsend.at[kind, t], xrecv.at[kind, t], dev(dx=dx)))

    def send_raw(kind, t, of, dx):
        ref, planes = chunk(t, of), sent_x(kind, t)

        def body(r):
            rows = pl.ds(r, 16)
            encode(ref[0, rows], ref[1, rows], planes, rows)

        by_rows(ROWS, body)
        send_x(kind, t, dx)

    def product(t):
        left = lhs[...].reshape(SLOTS * ROWS, 2 * TOK)
        if t < NY:
            b = lax.rem(y + offs[t], NY)

            @pl.loop(0, WIDE // 256)
            def _(n):
                cols = pl.ds(pl.multiple_of(n * 256, 256), 256)
                wide_p[t, :, :, cols] = lax.dot_general(
                    left, feats[b, cols, :], (((1,), (1,)), ((), ())),
                    preferred_element_type=F32).reshape(SLOTS, ROWS, 256)
        else:
            tail_p[...] = lax.dot_general(
                left, tailf[...], (((1,), (1,)), ((), ())),
                preferred_element_type=F32).reshape(SLOTS, ROWS, TAIL)
        send_raw(0, t, 2, step)
        send_raw(1, t, -step, -step)

    def recv(dst, sem):
        pltpu.make_async_remote_copy(
            src_ref=dst, dst_ref=dst, send_sem=sem, recv_sem=sem,
            device_id=dev(dc=1), device_id_type=MESH).wait_recv()

    def forward_sum(t):
        came, ref, planes = arrived_x(0, t), chunk(t, step), sent_x(2, t)
        recv(came, xrecv.at[0, t])

        def body(r):
            rows = pl.ds(r, 16)
            one, two = decode(came, rows)
            encode(ref[0, rows] + one, ref[1, rows] + two, planes, rows)

        by_rows(ROWS, body)
        send_x(2, t, step)

    def own_sum(t):
        ref, raw, summed = chunk(t, 0), arrived_x(1, t), arrived_x(2, t)
        planes, came = (out_z.at[t], got_z.at[t]) if t < NY else (tout_z, tgot_z)
        recv(raw, xrecv.at[1, t])
        recv(summed, xrecv.at[2, t])

        def body(r):
            rows = pl.ds(r, 16)
            one, two = decode(raw, rows)
            three, four = decode(summed, rows)
            ref[0, rows] = ref[0, rows] + one + three
            ref[1, rows] = ref[1, rows] + two + four

        by_rows(ROWS, body)
        given = ref.at[1 - h]

        def body_z(r):
            encode(given[pl.ds(r, 16)], given[pl.ds(r + ROWS // 2, 16)], planes, pl.ds(r, 16))

        by_rows(ROWS // 2, body_z)
        started.append(remote(planes, came, zsend.at[t], zrecv.at[t], dev(dh=1)))

    def finish(t):
        came = got_z.at[t] if t < NY else tgot_z
        dst = gsum.at[lax.rem(y + offs[t], NY)] if t < NY else tsum
        kept = chunk(t, 0).at[h]
        recv(came, zrecv.at[t])

        def body(r):
            one, two = decode(came, pl.ds(r, 16))
            dst[pl.ds(r, 16)] = kept[pl.ds(r, 16)] + one
            dst[pl.ds(r + ROWS // 2, 16)] = kept[pl.ds(r + ROWS // 2, 16)] + two

        by_rows(ROWS // 2, body)

    def sib_forward(t):
        b = lax.rem(y + offs[t], NY)
        started.append(remote(feats.at[b, :, mine], feats.at[b, :, mine],
                              csend.at[t], crecv.at[t], dev(dc=1)))

    def block(t):
        b = lax.rem(y + offs[t], NY)
        return feats.at[b, :, mine], feats.at[b, :, other]

    recv(block(0)[1], crecv.at[0])
    product(0)
    forward_sum(0)
    recv(block(1)[0], yrecv.at[1])
    recv(block(2)[0], yrecv.at[2])
    on = feats.at[lax.rem(y - step + NY, NY), :, mine]
    started.append(remote(on, on, ysend.at[2], yrecv.at[3], dev(dy=step)))
    sib_forward(1)
    sib_forward(2)
    recv(block(1)[1], crecv.at[1])
    product(1)
    recv(block(2)[1], crecv.at[2])
    product(2)
    own_sum(0)
    forward_sum(1)
    recv(block(3)[0], yrecv.at[3])
    sib_forward(3)
    forward_sum(2)
    recv(block(3)[1], crecv.at[3])
    product(3)
    tailf[...] = jnp.zeros_like(tailf)
    for b in range(NY):
        tailf[16 * b:16 * (b + 1)] = feats[b, WIDE:HELD]
    product(4)
    own_sum(1)
    finish(0)
    forward_sum(3)
    forward_sum(4)
    own_sum(2)
    finish(1)
    own_sum(3)
    own_sum(4)
    finish(2)
    finish(3)
    finish(4)

    decay = 1.0 - STEP ** (-DECAY_POWER)
    for b in range(NY):
        nat[:, BLOCK * b:BLOCK * b + WIDE] = gsum[b]
        nat[:, BLOCK * b + WIDE:BLOCK * (b + 1)] = tsum[:, 16 * b:16 * b + REST]
    squares = nat[...] * nat[...]
    row_mean = jnp.sum(squares + EPS_GRAD, axis=1, keepdims=True) / D
    eye = (lax.broadcasted_iota(jnp.int32, (ROWS, ROWS), 0)
           == lax.broadcasted_iota(jnp.int32, (ROWS, ROWS), 1))
    row_old = jnp.sum(jnp.where(eye, row_ref[...], 0.0), axis=1, keepdims=True)
    row_stat = decay * row_old + (1.0 - decay) * row_mean
    row_out[...] = jnp.sum(jnp.where(eye, row_stat, 0.0), axis=0, keepdims=True)
    slot_a = x * NC + c
    slot_b = y * NH + h
    stat_a[slot_a, 0:1] = jnp.sum(squares + EPS_GRAD, axis=0, keepdims=True)
    stat_a[slot_a, 1:2] = jnp.sum(squares / row_stat, axis=0, keepdims=True)
    for i, (dx, dc) in enumerate(group_a):
        started.append(remote(stat_a.at[slot_a], stat_a.at[slot_a], ssend.at[0, i], srecv.at[0, i],
                              dev(dx=dx, dc=dc)))
    for i, (dx, dc) in enumerate(group_a):
        recv(stat_a.at[lax.rem(x - dx + NX, NX) * NC + lax.rem(c + dc, NC)], srecv.at[0, i])
    stat_b[slot_b] = jnp.sum(stat_a[...], axis=0)
    for i, (dy, dh) in enumerate(group_b):
        started.append(remote(stat_b.at[slot_b], stat_b.at[slot_b], ssend.at[1, i], srecv.at[1, i],
                              dev(dy=dy, dh=dh)))
    for i, (dy, dh) in enumerate(group_b):
        recv(stat_b.at[lax.rem(y - dy + NY, NY) * NH + lax.rem(h + dh, NH)], srecv.at[1, i])
    sums = jnp.sum(stat_b[...], axis=0)
    load_m.wait()
    col_stat = decay * col_ref[...] + (1.0 - decay) * (sums[0:1] / FF)
    col_out[...] = col_stat
    update_rms = jnp.sqrt(jnp.sum(sums[1:2] / col_stat, axis=1, keepdims=True) / (FF * D))
    scale = 1.0 / jnp.maximum(1.0, update_rms)
    direction = nat[...] * lax.rsqrt(row_stat) * (lax.rsqrt(col_stat) * scale)
    dir_ref[...] = direction
    master_new = held_m[...] - LEARNING_RATE * direction
    new_ref[...] = master_new
    plain[:, 2048:2176] = jnp.zeros((ROWS, 128), BF16)
    plain[:, 0:D] = master_new.astype(BF16)

    rows_in[x, h, c] = plain[:, pl.ds(pl.multiple_of(c * HALF, HALF), HALF + EXTRA)]
    half = remote(plain.at[:, pl.ds(pl.multiple_of((1 - c) * HALF, HALF), HALF + EXTRA)],
                  rows_in.at[x, h, c], hsend.at[1], hrecv.at[1], dev(dc=1))
    half.wait()

    def each(p, body):
        if p < PARTS - 1:
            body()
        else:
            pl.when(c == 1)(body)

    def width(p):
        return (PART if p < PARTS - 1 else EXTRA)

    def piece(dx, dh, p):
        return rows_in.at[lax.rem(x + dx + NX, NX), lax.rem(h + dh, NH), :, :, pl.ds(PART * p, width(p))]

    waits = []
    back = -step

    def give_rows(kind, p, src_dx, dh, to):
        ref = piece(src_dx, dh, p)
        k = kind * PARTS + p
        pltpu.make_async_remote_copy(
            src_ref=ref, dst_ref=ref, send_sem=gsend.at[k], recv_sem=grecv.at[k],
            device_id=to, device_id_type=MESH).start()
        waits.append((p, k, lambda: piece(src_dx, dh, p)))

    def got(kind, dx, dh, p):
        recv(piece(dx, dh, p), grecv.at[kind * PARTS + p])

    def region(dx, p, core):
        size = PART if p < PARTS - 1 else D - 2 * HALF
        return (pl.ds(pl.multiple_of(core * HALF + PART * p, 32), size),
                pl.ds(pl.multiple_of(lax.rem(x + dx + NX, NX) * 384, 384), 384))

    def turn(i, dx, p):
        source = rows_in[lax.rem(x + dx + NX, NX), :, :, :, PART * p:PART * p + width(p)]
        value = source.reshape(NH * NC * ROWS, width(p)).T
        r, l = region(dx, p, c)
        params_ref[r, l] = value if p < PARTS - 1 else value[0:D - 2 * HALF]
        k = (7 + i) * PARTS + p
        ref = params_ref.at[r, l]
        pltpu.make_async_remote_copy(
            src_ref=ref, dst_ref=ref, send_sem=gsend.at[k], recv_sem=grecv.at[k],
            device_id=dev(dc=1), device_id_type=MESH).start()
        waits.append((p, k, lambda: params_ref.at[region(dx, p, c)]))

    for p in range(PARTS):
        def begin(p=p):
            give_rows(0, p, 0, 0, dev(dh=1))
            give_rows(1, p, 0, 0, dev(dx=1))
            give_rows(3, p, 0, 0, dev(dx=-1))
        each(p, begin)
    for p in range(PARTS):
        def middle(p=p):
            got(0, 0, 1, p)
            give_rows(2, p, 0, 1, dev(dx=1))
            give_rows(4, p, 0, 1, dev(dx=-1))
            turn(0, 0, p)
            got(1, -1, 0, p)
            got(3, 1, 0, p)
            give_rows(5, p, back, 0, dev(dx=step))
        each(p, middle)
    for p in range(PARTS):
        def late(p=p):
            got(2, -1, 1, p)
            got(4, 1, 1, p)
            give_rows(6, p, back, 1, dev(dx=step))
            turn(1, 1, p)
            turn(2, -1, p)
            got(5, 2, 0, p)
        each(p, late)
    for p in range(PARTS):
        def last(p=p):
            got(6, 2, 1, p)
            turn(3, 2, p)
        each(p, last)
    for p in range(PARTS):
        def shared(p=p):
            for i, dx in enumerate((0, 1, -1, 2)):
                r, l = region(dx, p, 1 - c)
                recv(params_ref.at[r, l], grecv.at[(7 + i) * PARTS + p])
        if p < PARTS - 1:
            shared()
        else:
            pl.when(c == 0)(shared)
    for p in range(PARTS):
        def sent(p=p):
            for q, k, of in waits:
                if q == p:
                    pltpu.make_async_remote_copy(
                        src_ref=of(), dst_ref=of(), send_sem=gsend.at[k], recv_sem=grecv.at[k],
                        device_id=dev(dc=1), device_id_type=MESH).wait_send()
        each(p, sent)
    for copy in started:
        copy.wait_send()


def local(hidden, out_grad, master, row_prev, col_prev):
    vmem = pl.BlockSpec(memory_space=pltpu.VMEM)
    anywhere = pl.BlockSpec(memory_space=pl.ANY)
    dma = pltpu.SemaphoreType.DMA
    params, master_new, direction, row_stat, col_stat = pl.pallas_call(
        kernel,
        out_shape=(
            pltpu.VMEM((D, NC * SLOTS * ROWS), BF16),
            pltpu.VMEM((ROWS, D), F32),
            pltpu.VMEM((ROWS, D), F32),
            pltpu.VMEM((1, ROWS), F32),
            pltpu.VMEM((1, D), F32),
        ),
        in_specs=[anywhere, anywhere, anywhere, vmem, vmem],
        out_specs=(vmem, vmem, vmem, vmem, vmem),
        scratch_shapes=[
            pltpu.VMEM((TOK, NC * SLOTS * ROWS), BF16),
            pltpu.VMEM((BLOCK, TOK), BF16),
            pltpu.VMEM((SLOTS, NC, ROWS, TOK), BF16),
            pltpu.VMEM((SLOTS, ROWS, NC * TOK), BF16),
            pltpu.VMEM((NY, HELD, NC * TOK), BF16),
            pltpu.VMEM((TAIL, NC * TOK), BF16),
            pltpu.VMEM((NY, SLOTS, ROWS, WIDE), F32),
            pltpu.VMEM((SLOTS, ROWS, TAIL), F32),
            pltpu.VMEM((3, NY, 3, ROWS, WIDE), BF16),
            pltpu.VMEM((NY, 3, ROWS // 2, WIDE), BF16),
            pltpu.VMEM((3, 3, ROWS, TAIL), BF16),
            pltpu.VMEM((3, ROWS // 2, TAIL), BF16),
            pltpu.VMEM((3, NY, 3, ROWS, WIDE), BF16),
            pltpu.VMEM((NY, 3, ROWS // 2, WIDE), BF16),
            pltpu.VMEM((3, 3, ROWS, TAIL), BF16),
            pltpu.VMEM((3, ROWS // 2, TAIL), BF16),
            pltpu.VMEM((NY, ROWS, WIDE), F32),
            pltpu.VMEM((ROWS, TAIL), F32),
            pltpu.VMEM((ROWS, D), F32),
            pltpu.VMEM((ROWS, D), F32),
            pltpu.VMEM((NX * NC, 2, D), F32),
            pltpu.VMEM((NY * NH, 2, D), F32),
            pltpu.VMEM((ROWS, HALF * 2 + EXTRA), BF16),
            pltpu.VMEM((NX, NH, NC, ROWS, HALF + EXTRA), BF16),
            dma((3,)), dma,
            dma((3,)), dma((4,)), dma((4,)), dma((4,)), dma((2,)), dma((2,)),
            dma((3, NB)), dma((3, NB)), dma((NB,)), dma((NB,)), dma((2, 7)), dma((2, 7)),
            dma((11 * PARTS,)), dma((11 * PARTS,)),
        ],
        compiler_params=pltpu.CompilerParams(
            collective_id=0, has_side_effects=True, vmem_limit_bytes=50 * 2**20),
        cost_estimate=pl.CostEstimate(
            flops=2 * TOK * FF // NY * D, bytes_accessed=16 * 2**20, transcendentals=0),
        name="factored_step",
    )(hidden[0], out_grad[0].T, master[0], row_prev, col_prev)
    return params.T[None], master_new[None], direction[None], row_stat, col_stat


def solution(mesh):
    in_specs = (
        P("expert", "dp", "mp"),
        P("expert", "dp", "mp"),
        P("expert", ("mp", "dp"), None),
        P("expert", ("mp", "dp")),
        P("expert", None),
    )
    out_specs = (
        P("expert", "mp", None),
        P("expert", ("mp", "dp"), None),
        P("expert", ("mp", "dp"), None),
        P("expert", ("mp", "dp")),
        P("expert", None),
    )
    return jax.shard_map(local, mesh=mesh, in_specs=in_specs, out_specs=out_specs, check_vma=False)
```

time: 157 us -> 128 us (0.82)
  Pallas kernels: 141 us -> 122 us
  local copies, waits for them, and re-layouts: 14.8 us -> 5.64 us
    pallas_call x1, Pallas kernels: 141 us -> 122 us  [local(): pl.pallas_call(kernel, out_shape=(pltpu.VMEM((D, NC * SLOTS * ROWS), BF16...]
    unnamed x14 -> x5, local copies, waits for them, and re-layouts: 14.8 us -> 5.64 us
where the time goes in v2:
time: 128 us
  Pallas kernels  122 us (95%)
  local copies, waits for them, and re-layouts  5.64 us (4%)
    pallas_call x1, Pallas kernels, local(): pl.pallas_call(kernel, out_shape=(pltpu.VMEM((D, NC * SLOTS * ROWS), BF16...  122 us
    unnamed x5, local copies, waits for them, and re-layouts  5.64 us

profile of v2, /device:TPU:33, one launch (start us, length us, event | category | flops | bytes accessed | tf_op | source)
XLA Modules:
  0.0 128.3 jit_solution(16591008967901414923)
XLA Ops:
  0.6 122.1 %factored_step.1 = (bf16[2080,1536]{1,0:T(8,128)(2,1)S(1)}, f32[96,2080]{1,0:T(8,128)S(1)}, f32[96,2080]{1,0:T(8,128)S(1)}, f32[1,96]{1,0:T(1,128)S(1)}, f32[1,2080]{1,0:T(1,128)S(1)}) custom-call(bf16[512,1536]{1,0:T(8,128)(2,1)} %bitcast.13, bf16[520,512]{1,0:T(8,128)(2,1)} %bitcast.15, f32[96,2080]{1,0:T(8,128)} %bitcast.14, f32[1,96]{1,0:T(1,128)} %row_ref.1, ...), custom_call_target="tpu_custom_call" | custom-call | flops 3271557120 | bytes 16777216 | tf_op jit(solution)/shard_map/factored_step/pallas_call | solution.py:423
  122.7 2.7 %copy.15 = bf16[1,1536,2080]{1,2,0:T(8,128)(2,1)} copy(bf16[1,1536,2080]{1,2,0:T(8,128)(2,1)S(1)} %bitcast.10) | data formatting | bytes 12779520
  125.4 0.9 copy.16
  126.3 0.5 copy.18
  126.9 0.6 copy.19
  127.5 0.9 copy.17

commit v3 on v0

v3 whole, which is shorter than its diff:
```python
import functools

import jax
import jax.numpy as jnp
from jax import lax
from jax.experimental import pallas as pl
from jax.experimental.pallas import tpu as pltpu
from jax.sharding import PartitionSpec as P

D = 2080
FF = 6144
STEP = 100
DECAY_POWER = 0.8
EPS_GRAD = 1e-30
LEARNING_RATE = 0.01

NX, NH, NC, NY = 4, 2, 2, 4
TOK = 512
ROWS = 96
SLOTS = NX * NH
WIDE = 512
BLOCK = D // NY
REST = BLOCK - WIDE
HELD = WIDE + 16
TAIL = 128
HALF = 1024
PART = 256
EXTRA = 128
PARTS = 5
MESH = pl.DeviceIdType.MESH
F32 = jnp.float32
BF16 = jnp.bfloat16

UNIT = 256
UNITS = NY * WIDE // UNIT

LEVELS = 21
REACH = 10.4 * 256
TINY = 1e-30


def last_place(wide):
    x = jnp.abs(wide) * 0.7515
    big = x * (2.0 ** 23 + 1.0)
    return big + (x - big)


def split(value, groups):
    high = value.astype(BF16)
    wide = high.astype(F32)
    if groups == 2:
        inverse = pl.reciprocal(jnp.maximum(jnp.abs(wide), TINY), approx=True)
        return high, jnp.round((value - wide) * (inverse * REACH))
    inverse = pl.reciprocal(jnp.maximum(last_place(wide), TINY), approx=True)
    step = jnp.floor((value - wide) * (inverse * 1024.0))
    return high, jnp.minimum(jnp.maximum(step, -4.0), 3.0)


def encode(values, planes, rows):
    groups = len(values)
    steps = []
    for i, value in enumerate(values):
        high, step = split(value, groups)
        planes[i, rows] = high
        steps.append(step)
    if groups == 2:
        low = steps[0] * LEVELS + steps[1]
    else:
        low = steps[0] * 64.0 + (steps[1] * 8.0 + (steps[2] + 36.0))
    planes[groups, rows] = low.astype(BF16)


def decode(groups, planes, rows):
    low = planes[groups, rows].astype(F32)
    wides = [planes[i, rows].astype(F32) for i in range(groups)]
    if groups == 2:
        step_1 = jnp.round(low * (1.0 / LEVELS))
        steps = (step_1, low - LEVELS * step_1)
        return [w + jnp.abs(w) * (q * (1.0 / REACH)) for w, q in zip(wides, steps)]
    step_1 = jnp.floor(low * (1.0 / 64))
    low = low - 64.0 * step_1
    step_2 = jnp.floor(low * (1.0 / 8))
    step_3 = low - 8.0 * step_2
    shifted = (step_1 + 0.5, step_2 - 3.5, step_3 - 3.5)
    return [w + last_place(w) * (q * (1.0 / 1024)) for w, q in zip(wides, shifted)]


GX, GZ = 3, 2
HALVES = (pl.ds(0, UNIT), pl.ds(UNIT, HELD - UNIT))
PAIR = NH * ROWS


def by_rows(count, body):
    @pl.loop(0, count // 16)
    def _(i):
        body(pl.multiple_of(i * 16, 16))


def kernel(hidden_ref, grad_ref, master_ref, row_ref, col_ref,
           params_ref, new_ref, dir_ref, row_out, col_out,
           hid, own_grad, turned, lhs, feats, tailf, wide_p, tail_p,
           out_x, out_z, tout_x, tout_z,
           got_x, got_z, tgot_x, tgot_z,
           gsum, tsum, nat, held_m, stat_a, stat_b, plain, rows_in,
           load_sem, copy_sem,
           ysend, yrecv, csend, crecv, hsend, hrecv,
           xsend, xrecv, zsend, zrecv, ssend, srecv,
           gsend, grecv, osend, orecv):
    dp, ex, y = lax.axis_index("dp"), lax.axis_index("expert"), lax.axis_index("mp")
    x, h, c = dp // 4, lax.rem(dp // 2, 2), lax.rem(dp, 2)
    step = 1 - 2 * c

    def dev(dx=0, dh=0, dc=0, dy=0):
        return (
            (lax.rem(x + dx + NX, NX) * NH + lax.rem(h + dh, NH)) * NC + lax.rem(c + dc, NC),
            ex,
            lax.rem(y + dy + NY, NY),
        )

    def remote(src, dst, send, recv, to):
        copy = pltpu.make_async_remote_copy(
            src_ref=src, dst_ref=dst, send_sem=send, recv_sem=recv,
            device_id=to, device_id_type=MESH)
        copy.start()
        return copy

    started = []

    load_h = pltpu.make_async_copy(hidden_ref, hid, load_sem.at[0])
    load_h.start()
    mine = pl.ds(pl.multiple_of(c * TOK, TOK), TOK)
    other = pl.ds(pl.multiple_of((1 - c) * TOK, TOK), TOK)
    load_g = pltpu.make_async_copy(grad_ref, own_grad, load_sem.at[1])
    load_g.start()
    load_m = pltpu.make_async_copy(master_ref, held_m, load_sem.at[2])
    load_m.start()

    group_a = [(dx, dc) for dx in range(NX) for dc in range(NC) if (dx, dc) != (0, 0)]
    group_b = [(dy, dh) for dy in range(NY) for dh in range(NH) if (dy, dh) != (0, 0)]
    barrier = pltpu.get_barrier_semaphore()
    for dx, dc in group_a:
        pl.semaphore_signal(barrier, 1, device_id=dev(dx=dx, dc=dc), device_id_type=MESH)
    for dy, dh in group_b:
        pl.semaphore_signal(barrier, 1, device_id=dev(dy=dy, dh=dh), device_id_type=MESH)

    load_h.wait()
    for g in range(4):
        part = hid[:, pl.ds(384 * g, 384)].T
        for q in range(4):
            turned[2 * g + q // 2, q % 2] = part[ROWS * q:ROWS * (q + 1), :]
    load_g.wait()
    feats[y, 0:WIDE, mine] = own_grad[0:WIDE, :]
    feats[y, WIDE:HELD, mine] = jnp.concatenate(
        [own_grad[WIDE:BLOCK, :], jnp.zeros((HELD - BLOCK, TOK), BF16)], axis=0)
    pl.semaphore_wait(barrier, len(group_a) + len(group_b))

    give_h = remote(turned.at[:, 1 - c], lhs.at[:, :, mine], hsend.at[0], hrecv.at[0], dev(dc=1))
    keep_h = pltpu.make_async_copy(turned.at[:, c], lhs.at[:, :, mine], copy_sem)
    keep_h.start()
    for i in range(2):
        own_i = feats.at[y, HALVES[i], mine]
        started.append(remote(own_i, own_i, csend.at[0, i], crecv.at[0, i], dev(dc=1)))
        started.append(remote(own_i, own_i, ysend.at[0, i], yrecv.at[2, i], dev(dy=1)))
        started.append(remote(own_i, own_i, ysend.at[1, i], yrecv.at[1, i], dev(dy=-1)))
    keep_h.wait()
    give_h.wait()

    offs = (0, 1, 3, 2)
    last = UNITS

    def sent_x(kind, u):
        return out_x.at[kind, u] if u < last else tout_x.at[kind]

    def arrived_x(kind, u):
        return got_x.at[kind, u] if u < last else tgot_x.at[kind]

    def chunk(u, dx):
        return (wide_p.at[u] if u < last else tail_p).at[lax.rem(x + dx + NX, NX)]

    def height(u):
        return PAIR if u < last else ROWS

    def times(left, right):
        return lax.dot_general(left, right, (((1,), (1,)), ((), ())), preferred_element_type=F32)

    def send_x(kind, u, dx):
        started.append(remote(sent_x(kind, u), arrived_x(kind, u),
                              xsend.at[kind, u], xrecv.at[kind, u], dev(dx=dx)))

    def spans(groups, total, r):
        return [pl.ds(i * (total // groups) + r, 16) for i in range(groups)]

    def send_raw(kind, u, of, dx):
        ref, planes = chunk(u, of), sent_x(kind, u)

        def body(r):
            encode([ref[rows] for rows in spans(GX, height(u), r)], planes, pl.ds(r, 16))

        by_rows(height(u) // GX, body)
        send_x(kind, u, dx)

    def product(u):
        if u < last:
            block, first = lax.rem(y + offs[u // 2], NY), UNIT * (u % 2)

        @pl.loop(0, NX)
        def _(i):
            if u < last:
                left = lhs[pl.ds(2 * i, 2)].reshape(PAIR, 2 * TOK)
                wide_p[u, i] = times(left, feats[block, first:first + UNIT, :])
            else:
                tail_p[i] = times(lhs[2 * i], tailf[0]) + times(lhs[2 * i + 1], tailf[1])

        send_raw(0, u, 2, step)
        send_raw(1, u, -step, -step)

    def recv(dst, sem):
        pltpu.make_async_remote_copy(
            src_ref=dst, dst_ref=dst, send_sem=sem, recv_sem=sem,
            device_id=dev(dc=1), device_id_type=MESH).wait_recv()

    def forward_sum(u):
        came, ref, planes = arrived_x(0, u), chunk(u, step), sent_x(2, u)
        recv(came, xrecv.at[0, u])

        def body(r):
            rows = pl.ds(r, 16)
            more = decode(GX, came, rows)
            encode([ref[at] + m for at, m in zip(spans(GX, height(u), r), more)], planes, rows)

        by_rows(height(u) // GX, body)
        send_x(2, u, step)

    def own_sum(u):
        ref, raw, summed = chunk(u, 0), arrived_x(1, u), arrived_x(2, u)
        planes, came = (out_z.at[u], got_z.at[u]) if u < last else (tout_z, tgot_z)
        recv(raw, xrecv.at[1, u])
        recv(summed, xrecv.at[2, u])

        def body(r):
            rows = pl.ds(r, 16)
            one, two = decode(GX, raw, rows), decode(GX, summed, rows)
            for at, m, n in zip(spans(GX, height(u), r), one, two):
                ref[at] = ref[at] + m + n

        by_rows(height(u) // GX, body)
        given = ref.at[pl.ds(pl.multiple_of((1 - h) * ROWS, ROWS), ROWS)] if u < last else ref

        def body_z(r):
            encode([given[at] for at in spans(GZ, ROWS, r)], planes, pl.ds(r, 16))

        by_rows(ROWS // GZ, body_z)
        started.append(remote(planes, came, zsend.at[u], zrecv.at[u], dev(dh=1)))

    def finish(u):
        came = got_z.at[u] if u < last else tgot_z
        dst = gsum.at[lax.rem(y + offs[u // 2], NY), u % 2] if u < last else tsum
        kept = chunk(u, 0)
        if u < last:
            kept = kept.at[pl.ds(pl.multiple_of(h * ROWS, ROWS), ROWS)]
        recv(came, zrecv.at[u])

        def body(r):
            for at, m in zip(spans(GZ, ROWS, r), decode(GZ, came, pl.ds(r, 16))):
                dst[at] = kept[at] + m

        by_rows(ROWS // GZ, body)

    def half_block(t, i, tokens):
        return feats.at[lax.rem(y + offs[t], NY), HALVES[i], tokens]

    def to_sibling(t, i):
        ref = half_block(t, i, mine)
        started.append(remote(ref, ref, csend.at[t, i], crecv.at[t, i], dev(dc=1)))

    def neighbours(i):
        recv(half_block(1, i, mine), yrecv.at[1, i])
        recv(half_block(2, i, mine), yrecv.at[2, i])
        on = feats.at[lax.rem(y - step + NY, NY), HALVES[i], mine]
        started.append(remote(on, on, ysend.at[2, i], yrecv.at[3, i], dev(dy=step)))
        to_sibling(1, i)
        to_sibling(2, i)

    def opposite(i):
        recv(half_block(3, i, mine), yrecv.at[3, i])
        to_sibling(3, i)

    def compute(t, i):
        recv(half_block(t, i, other), crecv.at[t, i])
        product(2 * t + i)

    def tail():
        tailf[...] = jnp.zeros_like(tailf)
        for b in range(NY):
            tailf[0, 16 * b:16 * (b + 1)] = feats[b, WIDE:HELD]
            tailf[1, 64 + 16 * b:64 + 16 * (b + 1)] = feats[b, WIDE:HELD]
        product(last)

    compute(0, 0)
    compute(0, 1)
    forward_sum(0)
    neighbours(0)
    compute(1, 0)
    compute(2, 0)
    forward_sum(1)
    own_sum(0)
    neighbours(1)
    compute(1, 1)
    compute(2, 1)
    forward_sum(2)
    opposite(0)
    compute(3, 0)
    own_sum(1)
    forward_sum(4)
    opposite(1)
    compute(3, 1)
    tail()
    forward_sum(3)
    own_sum(2)
    forward_sum(5)
    finish(0)
    own_sum(4)
    forward_sum(6)
    finish(1)
    own_sum(3)
    forward_sum(7)
    forward_sum(8)
    own_sum(5)
    finish(2)
    own_sum(6)
    finish(4)
    finish(3)
    own_sum(7)
    own_sum(8)
    finish(5)
    finish(6)
    finish(7)
    finish(8)

    decay = 1.0 - STEP ** (-DECAY_POWER)
    ends = jnp.where(h == 0, tsum[:, 0:64], tsum[:, 64:128])
    for b in range(NY):
        for i in range(2):
            nat[:, BLOCK * b + UNIT * i:BLOCK * b + UNIT * (i + 1)] = gsum[b, i]
        nat[:, BLOCK * b + WIDE:BLOCK * (b + 1)] = ends[:, 16 * b:16 * b + REST]
    squares = nat[...] * nat[...]
    row_mean = jnp.sum(squares + EPS_GRAD, axis=1, keepdims=True) / D
    eye = (lax.broadcasted_iota(jnp.int32, (ROWS, ROWS), 0)
           == lax.broadcasted_iota(jnp.int32, (ROWS, ROWS), 1))
    row_old = jnp.sum(jnp.where(eye, row_ref[...], 0.0), axis=1, keepdims=True)
    row_stat = decay * row_old + (1.0 - decay) * row_mean
    row_out[...] = jnp.sum(jnp.where(eye, row_stat, 0.0), axis=0, keepdims=True)
    slot_a = x * NC + c
    slot_b = y * NH + h
    stat_a[slot_a, 0:1] = jnp.sum(squares + EPS_GRAD, axis=0, keepdims=True)
    stat_a[slot_a, 1:2] = jnp.sum(squares / row_stat, axis=0, keepdims=True)
    for i, (dx, dc) in enumerate(group_a):
        started.append(remote(stat_a.at[slot_a], stat_a.at[slot_a], ssend.at[0, i], srecv.at[0, i],
                              dev(dx=dx, dc=dc)))
    for i, (dx, dc) in enumerate(group_a):
        recv(stat_a.at[lax.rem(x - dx + NX, NX) * NC + lax.rem(c + dc, NC)], srecv.at[0, i])
    stat_b[slot_b] = jnp.sum(stat_a[...], axis=0)
    for i, (dy, dh) in enumerate(group_b):
        started.append(remote(stat_b.at[slot_b], stat_b.at[slot_b], ssend.at[1, i], srecv.at[1, i],
                              dev(dy=dy, dh=dh)))
    for i, (dy, dh) in enumerate(group_b):
        recv(stat_b.at[lax.rem(y - dy + NY, NY) * NH + lax.rem(h + dh, NH)], srecv.at[1, i])
    sums = jnp.sum(stat_b[...], axis=0)
    load_m.wait()
    col_stat = decay * col_ref[...] + (1.0 - decay) * (sums[0:1] / FF)
    col_out[...] = col_stat
    update_rms = jnp.sqrt(jnp.sum(sums[1:2] / col_stat, axis=1, keepdims=True) / (FF * D))
    scale = 1.0 / jnp.maximum(1.0, update_rms)
    direction = nat[...] * lax.rsqrt(row_stat) * (lax.rsqrt(col_stat) * scale)
    dir_ref[...] = direction
    master_new = held_m[...] - LEARNING_RATE * direction
    new_ref[...] = master_new
    plain[:, 2048:2176] = jnp.zeros((ROWS, 128), BF16)
    plain[:, 0:D] = master_new.astype(BF16)

    rows_in[x, h, c] = plain[:, pl.ds(pl.multiple_of(c * HALF, HALF), HALF + EXTRA)]

    def whole(body):
        @pl.loop(0, PARTS - 1)
        def _(p):
            body(p, PART)

    def rest(body):
        @pl.when(c == 1)
        def _():
            body(PARTS - 1, EXTRA)

    def start_of(p):
        return PART * p if isinstance(p, int) else pl.multiple_of(p * PART, PART)

    def piece(dx, dh, p, width):
        return rows_in.at[lax.rem(x + dx + NX, NX), lax.rem(h + dh, NH), :, :, pl.ds(start_of(p), width)]

    def region(dx, p, core, width):
        size = width if width == PART else D - 2 * HALF
        return params_ref.at[
            pl.ds(pl.multiple_of(core * HALF + p * PART, 256 if width == PART else 1024), size),
            pl.ds(pl.multiple_of(lax.rem(x + dx + NX, NX) * 384, 384), 384)]

    def give(ref, kind, p, to):
        pltpu.make_async_remote_copy(
            src_ref=ref, dst_ref=ref, send_sem=gsend.at[kind, p], recv_sem=grecv.at[kind, p],
            device_id=to, device_id_type=MESH).start()

    def got(ref, kind, p):
        recv(ref, grecv.at[kind, p])

    def given(ref, kind, p):
        pltpu.make_async_remote_copy(
            src_ref=ref, dst_ref=ref, send_sem=gsend.at[kind, p], recv_sem=grecv.at[kind, p],
            device_id=dev(dc=1), device_id_type=MESH).wait_send()

    def turn(i, dx, p, width):
        ref = region(dx, p, c, width)
        for j in range(0, width, 128):
            at = j + start_of(p)
            at = at if isinstance(p, int) else pl.multiple_of(at, 128)
            value = rows_in[lax.rem(x + dx + NX, NX), :, :, :, pl.ds(at, 128)].reshape(NH * NC * ROWS, 128).T
            if width == PART:
                ref[j:j + 128, :] = value
            else:
                ref[...] = value[0:D - 2 * HALF]
        give(ref, 7 + i, p, dev(dc=1))

    ways = [(kind, k, to) for kind, to in enumerate((dict(dh=1), dict(dx=1), dict(dx=-1), dict()))
            for k in range(2) if (to or k)]

    def own_rows(p, width, kind, k, to):
        core = c if k == 0 else 1 - c
        src = plain.at[:, pl.ds(pl.multiple_of(core * HALF + start_of(p), 128), width)]
        return pltpu.make_async_remote_copy(
            src_ref=src, dst_ref=rows_in.at[x, h, c, :, pl.ds(start_of(p), width)],
            send_sem=osend.at[kind, k, p], recv_sem=orecv.at[kind, c, p],
            device_id=dev(dc=k, **to), device_id_type=MESH)

    def got_own(p, width, kind, dx, dh, owner):
        recv(rows_in.at[lax.rem(x + dx + NX, NX), lax.rem(h + dh, NH), owner, :, pl.ds(start_of(p), width)],
             orecv.at[kind, owner, p])

    def begin(p, width):
        for kind, k, to in ways:
            own_rows(p, width, kind, k, to).start()

    def begun(p, width):
        for kind, k, to in ways:
            own_rows(p, width, kind, k, to).wait_send()

    def middle(p, width):
        for owner in range(NC):
            got_own(p, width, 0, 0, 1, owner)
        ref = piece(0, 1, p, width)
        give(ref, 2, p, dev(dx=1))
        give(ref, 4, p, dev(dx=-1))
        for owner in range(NC):
            got_own(p, width, 1, -1, 0, owner)
            got_own(p, width, 2, 1, 0, owner)
        give(piece(-step, 0, p, width), 5, p, dev(dx=step))
        got_own(p, width, 3, 0, 0, 1 - c)
        turn(0, 0, p, width)

    def late(p, width):
        got(piece(-1, 1, p, width), 2, p)
        got(piece(1, 1, p, width), 4, p)
        give(piece(-step, 1, p, width), 6, p, dev(dx=step))
        turn(1, 1, p, width)
        turn(2, -1, p, width)

    def final(p, width):
        got(piece(2, 0, p, width), 5, p)
        got(piece(2, 1, p, width), 6, p)
        turn(3, 2, p, width)

    def shared(p, width):
        for i, dx in enumerate((0, 1, -1, 2)):
            got(region(dx, p, 1 - c, width), 7 + i, p)

    def sent(p, width):
        for kind, dx, dh in ((2, 0, 1), (4, 0, 1), (5, -step, 0), (6, -step, 1)):
            given(piece(dx, dh, p, width), kind, p)
        for i, dx in enumerate((0, 1, -1, 2)):
            given(region(dx, p, c, width), 7 + i, p)

    def extra_begin(body):
        for k in range(2):
            @pl.when(c == 1 - k)
            def _():
                for kind, k_, to in ways:
                    if k_ == k:
                        body(own_rows(PARTS - 1, EXTRA, kind, k, to))

    extra_begin(lambda copy: copy.start())
    whole(begin)
    for body in (middle, late, final):
        rest(body)
        whole(body)
    whole(shared)
    pl.when(c == 0)(lambda: shared(PARTS - 1, EXTRA))
    whole(sent)
    rest(sent)
    whole(begun)
    extra_begin(lambda copy: copy.wait_send())
    for copy in started:
        copy.wait_send()


def write(*refs):
    sem = refs[-1]
    copies = [pltpu.make_async_copy(refs[i], refs[i + 5], sem.at[i]) for i in range(5)]
    for copy in copies:
        copy.start()
    for copy in copies:
        copy.wait()


def local(hidden, out_grad, master, row_prev, col_prev):
    vmem = pl.BlockSpec(memory_space=pltpu.VMEM)
    anywhere = pl.BlockSpec(memory_space=pl.ANY)
    dma = pltpu.SemaphoreType.DMA
    results = pl.pallas_call(
        kernel,
        out_shape=(
            pltpu.VMEM((D, NC * SLOTS * ROWS), BF16),
            pltpu.VMEM((ROWS, D), F32),
            pltpu.VMEM((ROWS, D), F32),
            pltpu.VMEM((1, ROWS), F32),
            pltpu.VMEM((1, D), F32),
        ),
        in_specs=[anywhere, anywhere, anywhere, vmem, vmem],
        out_specs=(vmem, vmem, vmem, vmem, vmem),
        scratch_shapes=[
            pltpu.VMEM((TOK, NC * SLOTS * ROWS), BF16),
            pltpu.VMEM((BLOCK, TOK), BF16),
            pltpu.VMEM((SLOTS, NC, ROWS, TOK), BF16),
            pltpu.VMEM((SLOTS, ROWS, NC * TOK), BF16),
            pltpu.VMEM((NY, HELD, NC * TOK), BF16),
            pltpu.VMEM((NH, TAIL, NC * TOK), BF16),
            pltpu.VMEM((UNITS, NX, PAIR, UNIT), F32),
            pltpu.VMEM((NX, ROWS, TAIL), F32),
            pltpu.VMEM((3, UNITS, GX + 1, PAIR // GX, UNIT), BF16),
            pltpu.VMEM((UNITS, GZ + 1, ROWS // GZ, UNIT), BF16),
            pltpu.VMEM((3, GX + 1, ROWS // GX, TAIL), BF16),
            pltpu.VMEM((GZ + 1, ROWS // GZ, TAIL), BF16),
            pltpu.VMEM((3, UNITS, GX + 1, PAIR // GX, UNIT), BF16),
            pltpu.VMEM((UNITS, GZ + 1, ROWS // GZ, UNIT), BF16),
            pltpu.VMEM((3, GX + 1, ROWS // GX, TAIL), BF16),
            pltpu.VMEM((GZ + 1, ROWS // GZ, TAIL), BF16),
            pltpu.VMEM((NY, 2, ROWS, UNIT), F32),
            pltpu.VMEM((ROWS, TAIL), F32),
            pltpu.VMEM((ROWS, D), F32),
            pltpu.VMEM((ROWS, D), F32),
            pltpu.VMEM((NX * NC, 2, D), F32),
            pltpu.VMEM((NY * NH, 2, D), F32),
            pltpu.VMEM((ROWS, HALF * 2 + EXTRA), BF16),
            pltpu.VMEM((NX, NH, NC, ROWS, HALF + EXTRA), BF16),
            dma((3,)), dma,
            dma((3, 2)), dma((4, 2)), dma((4, 2)), dma((4, 2)), dma((1,)), dma((1,)),
            dma((3, UNITS + 1)), dma((3, UNITS + 1)), dma((UNITS + 1,)), dma((UNITS + 1,)),
            dma((2, 7)), dma((2, 7)),
            dma((11, PARTS)), dma((11, PARTS)), dma((4, 2, PARTS)), dma((4, 2, PARTS)),
        ],
        compiler_params=pltpu.CompilerParams(
            collective_id=0, has_side_effects=True, vmem_limit_bytes=50 * 2**20),
        cost_estimate=pl.CostEstimate(
            flops=2 * TOK * FF // NY * D, bytes_accessed=16 * 2**20, transcendentals=0),
        name="factored_step",
    )(hidden[0], out_grad[0].T, master[0], row_prev, col_prev)
    params, master_new, direction, row_stat, col_stat = pl.pallas_call(
        write,
        out_shape=[pltpu.HBM(r.shape, r.dtype) for r in results],
        in_specs=[vmem] * 5,
        out_specs=[pl.BlockSpec(memory_space=pltpu.HBM)] * 5,
        scratch_shapes=[dma((5,))],
        compiler_params=pltpu.CompilerParams(vmem_limit_bytes=2 * 2**20),
        name="write_results",
    )(*[pltpu.with_memory_space_constraint(r, pltpu.VMEM) for r in results])
    return params.T[None], master_new[None], direction[None], row_stat, col_stat


def solution(mesh):
    in_specs = (
        P("expert", "dp", "mp"),
        P("expert", "dp", "mp"),
        P("expert", ("mp", "dp"), None),
        P("expert", ("mp", "dp")),
        P("expert", None),
    )
    out_specs = (
        P("expert", "mp", None),
        P("expert", ("mp", "dp"), None),
        P("expert", ("mp", "dp"), None),
        P("expert", ("mp", "dp")),
        P("expert", None),
    )
    return jax.shard_map(local, mesh=mesh, in_specs=in_specs, out_specs=out_specs, check_vma=False)
```

time: 953 us -> 122 us (0.13)
  blocking collectives: 591 us -> 0 us
  waiting for transfers between devices: 322 us -> 0 us
  Pallas kernels: 0 us -> 121 us
  between operations: 14.5 us -> 0.64 us
  local copies, waits for them, and re-layouts: 10.9 us -> 0 us
    psum x2 -> x0, blocking collectives: 591 us -> none  [the longest x1 389 us: joint_stats(): return lax.psum(stat_values, ('dp', 'mp'))]
    reduce_scatter x1 -> x0, waiting for transfers between devices: 178 us -> none  [local(): lax.psum_scatter(lax.dot_general(local_hidden, features, CONTRACT_TOKENS,...]
    all_gather x2 -> x0, waiting for transfers between devices: 143 us -> none  [the longest x1 104 us: local(): lax.all_gather(master_new.astype(jnp.bfloat16), 'dp', axis=0, tiled=True)]
    pallas_call x0 -> x2, Pallas kernels: none -> 121 us  [the longest x1 118 us: local(): pl.pallas_call(kernel, out_shape=(pltpu.VMEM((D, NC * SLOTS * ROWS), BF16...]
    unnamed x11 -> x0, local copies, waits for them, and re-layouts: 10.3 us -> none
  transfers between devices with their start and end apart: 3 -> 0, of which waited for: 3 -> 0; matrix products, arithmetic and copies ran while one was open for 0% -> 0% of each run, Pallas kernels for 0% -> 0%
where the time goes in v3:
time: 122 us
  Pallas kernels  121 us (99%)
    pallas_call x1, Pallas kernels, local(): pl.pallas_call(kernel, out_shape=(pltpu.VMEM((D, NC * SLOTS * ROWS), BF16...  118 us
    pallas_call x1, Pallas kernels, local(): pl.pallas_call(write, out_shape=[pltpu.HBM(r.shape, r.dtype) for r in res...  3.3 us

profile of v3, /device:TPU:1, one launch (start us, length us, event | category | flops | bytes accessed | tf_op | source)
XLA Modules:
  0.0 121.8 jit_solution(14409865261625901118)
XLA Ops:
  0.6 117.9 %factored_step.1 = (bf16[2080,1536]{1,0:T(8,128)(2,1)S(1)}, f32[96,2080]{1,0:T(8,128)S(1)}, f32[96,2080]{1,0:T(8,128)S(1)}, f32[1,96]{1,0:T(1,128)S(1)}, f32[1,2080]{1,0:T(1,128)S(1)}) custom-call(bf16[512,1536]{1,0:T(8,128)(2,1)} %bitcast.11, bf16[520,512]{1,0:T(8,128)(2,1)} %bitcast.15, f32[96,2080]{1,0:T(8,128)} %bitcast.12, f32[1,96]{1,0:T(1,128)} %row_ref.1, ...), custom_call_target="tpu_custom_call" | custom-call | flops 3271557120 | bytes 16777216 | tf_op jit(solution)/shard_map/factored_step/pallas_call | solution.py:524
  118.5 3.3 %write_results.1 = (bf16[2080,1536]{1,0:T(8,128)(2,1)}, f32[96,2080]{1,0:T(8,128)}, f32[96,2080]{1,0:T(8,128)}, f32[1,96]{1,0:T(1,128)}, f32[1,2080]{1,0:T(1,128)}) custom-call(bf16[2080,1536]{1,0:T(8,128)(2,1)S(1)} %get-tuple-element.15.refs_0_, f32[96,2080]{1,0:T(8,128)S(1)} %get-tuple-element.16.refs_1_, f32[96,2080]{1,0:T(8,128)S(1)} %get-tuple-element.17.refs_2_, ...), custom_call_target="tpu_custom_call" | custom-call | tf_op jit(solution)/shard_map/write_results/pallas_call | solution.py:572

commit v4 on v3

--- a/solution.py
+++ b/solution.py
@@ -27,6 +27,7 @@
 PART = 256
 EXTRA = 128
 PARTS = 5
+MIXED = 1
 MESH = pl.DeviceIdType.MESH
 F32 = jnp.float32
 BF16 = jnp.bfloat16
@@ -466,12 +467,25 @@
     def late(p, width):
         got(piece(-1, 1, p, width), 2, p)
         got(piece(1, 1, p, width), 4, p)
-        give(piece(-step, 1, p, width), 6, p, dev(dx=step))
+
+        def along_x():
+            give(piece(-step, 1, p, width), 6, p, dev(dx=step))
+
+        if width == PART:
+            pl.when(p >= MIXED)(along_x)
+        else:
+            along_x()
         turn(1, 1, p, width)
         turn(2, -1, p, width)
 
     def final(p, width):
-        got(piece(2, 0, p, width), 5, p)
+        def across():
+            got(piece(2, 0, p, width), 5, p)
+
+        if width == PART:
+            pl.when(p >= MIXED)(across)
+        else:
+            across()
         got(piece(2, 1, p, width), 6, p)
         turn(3, 2, p, width)
 
@@ -495,7 +509,12 @@
 
     extra_begin(lambda copy: copy.start())
     whole(begin)
-    for body in (middle, late, final):
+    rest(middle)
+    whole(middle)
+    for p in range(MIXED):
+        got(piece(2, 0, p, PART), 5, p)
+        give(piece(2, 0, p, PART), 6, p, dev(dh=1))
+    for body in (late, final):
         rest(body)
         whole(body)
     whole(shared)

time: 122 us -> 121 us (level)
  no operation moved by 1% of the time
where the time goes in v4:
time: 121 us
  Pallas kernels  120 us (99%)
    pallas_call x1, Pallas kernels, local(): pl.pallas_call(kernel, out_shape=(pltpu.VMEM((D, NC * SLOTS * ROWS), BF16...  117 us
    pallas_call x1, Pallas kernels, local(): pl.pallas_call(write, out_shape=[pltpu.HBM(r.shape, r.dtype) for r in res...  3.3 us

profile of v4, /device:TPU:1, one launch (start us, length us, event | category | flops | bytes accessed | tf_op | source)
XLA Modules:
  0.0 120.7 jit_solution(10442537274367904707)
XLA Ops:
  0.6 116.8 %factored_step.1 = (bf16[2080,1536]{1,0:T(8,128)(2,1)S(1)}, f32[96,2080]{1,0:T(8,128)S(1)}, f32[96,2080]{1,0:T(8,128)S(1)}, f32[1,96]{1,0:T(1,128)S(1)}, f32[1,2080]{1,0:T(1,128)S(1)}) custom-call(bf16[512,1536]{1,0:T(8,128)(2,1)} %bitcast.11, bf16[520,512]{1,0:T(8,128)(2,1)} %bitcast.15, f32[96,2080]{1,0:T(8,128)} %bitcast.12, f32[1,96]{1,0:T(1,128)} %row_ref.1, ...), custom_call_target="tpu_custom_call" | custom-call | flops 3271557120 | bytes 16777216 | tf_op jit(solution)/shard_map/factored_step/pallas_call | solution.py:543
  117.4 3.3 %write_results.1 = (bf16[2080,1536]{1,0:T(8,128)(2,1)}, f32[96,2080]{1,0:T(8,128)}, f32[96,2080]{1,0:T(8,128)}, f32[1,96]{1,0:T(1,128)}, f32[1,2080]{1,0:T(1,128)}) custom-call(bf16[2080,1536]{1,0:T(8,128)(2,1)S(1)} %get-tuple-element.15.refs_0_, f32[96,2080]{1,0:T(8,128)S(1)} %get-tuple-element.16.refs_1_, f32[96,2080]{1,0:T(8,128)S(1)} %get-tuple-element.17.refs_2_, ...), custom_call_target="tpu_custom_call" | custom-call | tf_op jit(solution)/shard_map/write_results/pallas_call | solution.py:591

commit v5 on v4

--- a/solution.py
+++ b/solution.py
@@ -26,6 +26,7 @@
 HALF = 1024
 PART = 256
 EXTRA = 128
+OVER = D - 2 * HALF
 PARTS = 5
 MIXED = 1
 MESH = pl.DeviceIdType.MESH
@@ -102,7 +103,7 @@
            hid, own_grad, turned, lhs, feats, tailf, wide_p, tail_p,
            out_x, out_z, tout_x, tout_z,
            got_x, got_z, tgot_x, tgot_z,
-           gsum, tsum, nat, held_m, stat_a, stat_b, plain, rows_in,
+           gsum, tsum, nat, held_m, stat_a, stat_b, plain, rows_in, plain_e, rows_e, wide_e,
            load_sem, copy_sem,
            ysend, yrecv, csend, crecv, hsend, hrecv,
            xsend, xrecv, zsend, zrecv, ssend, srecv,
@@ -204,13 +205,16 @@
         if u < last:
             block, first = lax.rem(y + offs[u // 2], NY), UNIT * (u % 2)
 
-        @pl.loop(0, NX)
+        @pl.loop(0, NX // 2)
         def _(i):
             if u < last:
-                left = lhs[pl.ds(2 * i, 2)].reshape(PAIR, 2 * TOK)
-                wide_p[u, i] = times(left, feats[block, first:first + UNIT, :])
+                left = lhs[pl.ds(4 * i, 4)].reshape(2 * PAIR, 2 * TOK)
+                wide_p[u, pl.ds(2 * i, 2)] = times(
+                    left, feats[block, first:first + UNIT, :]).reshape(2, PAIR, UNIT)
             else:
-                tail_p[i] = times(lhs[2 * i], tailf[0]) + times(lhs[2 * i + 1], tailf[1])
+                for j in range(2):
+                    at = 2 * i + j
+                    tail_p[at] = times(lhs[2 * at], tailf[0]) + times(lhs[2 * at + 1], tailf[1])
 
         send_raw(0, u, 2, step)
         send_raw(1, u, -step, -step)
@@ -376,10 +380,14 @@
     dir_ref[...] = direction
     master_new = held_m[...] - LEARNING_RATE * direction
     new_ref[...] = master_new
-    plain[:, 2048:2176] = jnp.zeros((ROWS, 128), BF16)
-    plain[:, 0:D] = master_new.astype(BF16)
-
-    rows_in[x, h, c] = plain[:, pl.ds(pl.multiple_of(c * HALF, HALF), HALF + EXTRA)]
+    plain[...] = master_new[:, 0:2 * HALF].astype(BF16)
+    nat[...] = master_new
+    padded = jnp.concatenate([nat[:, 2 * HALF:D], jnp.zeros((ROWS, 128 - OVER), F32)], axis=1)
+    plain_e[...] = jnp.zeros_like(plain_e)
+    plain_e[:, 0:ROWS] = padded.T[0:OVER, :].astype(BF16)
+    rows_e[x, h, c] = plain_e[...]
+
+    rows_in[x, h, c] = plain[:, pl.ds(pl.multiple_of(c * HALF, HALF), HALF)]
 
     def whole(body):
         @pl.loop(0, PARTS - 1)
@@ -395,6 +403,8 @@
         return PART * p if isinstance(p, int) else pl.multiple_of(p * PART, PART)
 
     def piece(dx, dh, p, width):
+        if width == EXTRA:
+            return rows_e.at[lax.rem(x + dx + NX, NX), lax.rem(h + dh, NH)]
         return rows_in.at[lax.rem(x + dx + NX, NX), lax.rem(h + dh, NH), :, :, pl.ds(start_of(p), width)]
 
     def region(dx, p, core, width):
@@ -418,14 +428,15 @@
 
     def turn(i, dx, p, width):
         ref = region(dx, p, c, width)
-        for j in range(0, width, 128):
-            at = j + start_of(p)
-            at = at if isinstance(p, int) else pl.multiple_of(at, 128)
+        if width == EXTRA:
+            for q in range(NH * NC):
+                wide_e[:, ROWS * q:ROWS * (q + 1)] = rows_e[
+                    lax.rem(x + dx + NX, NX), q // NC, q % NC][:, 0:ROWS].astype(F32)
+            ref[...] = wide_e[...].astype(BF16)
+        for j in range(0, width if width == PART else 0, 128):
+            at = pl.multiple_of(j + start_of(p), 128)
             value = rows_in[lax.rem(x + dx + NX, NX), :, :, :, pl.ds(at, 128)].reshape(NH * NC * ROWS, 128).T
-            if width == PART:
-                ref[j:j + 128, :] = value
-            else:
-                ref[...] = value[0:D - 2 * HALF]
+            ref[j:j + 128, :] = value
         give(ref, 7 + i, p, dev(dc=1))
 
     ways = [(kind, k, to) for kind, to in enumerate((dict(dh=1), dict(dx=1), dict(dx=-1), dict()))
@@ -433,15 +444,20 @@
 
     def own_rows(p, width, kind, k, to):
         core = c if k == 0 else 1 - c
-        src = plain.at[:, pl.ds(pl.multiple_of(core * HALF + start_of(p), 128), width)]
+        if width == EXTRA:
+            src, dst = plain_e, rows_e.at[x, h, c]
+        else:
+            src = plain.at[:, pl.ds(pl.multiple_of(core * HALF + start_of(p), 128), width)]
+            dst = rows_in.at[x, h, c, :, pl.ds(start_of(p), width)]
         return pltpu.make_async_remote_copy(
-            src_ref=src, dst_ref=rows_in.at[x, h, c, :, pl.ds(start_of(p), width)],
+            src_ref=src, dst_ref=dst,
             send_sem=osend.at[kind, k, p], recv_sem=orecv.at[kind, c, p],
             device_id=dev(dc=k, **to), device_id_type=MESH)
 
     def got_own(p, width, kind, dx, dh, owner):
-        recv(rows_in.at[lax.rem(x + dx + NX, NX), lax.rem(h + dh, NH), owner, :, pl.ds(start_of(p), width)],
-             orecv.at[kind, owner, p])
+        at = (lax.rem(x + dx + NX, NX), lax.rem(h + dh, NH), owner)
+        ref = rows_e.at[at] if width == EXTRA else rows_in.at[(*at, slice(None), pl.ds(start_of(p), width))]
+        recv(ref, orecv.at[kind, owner, p])
 
     def begin(p, width):
         for kind, k, to in ways:
@@ -574,8 +590,11 @@
             pltpu.VMEM((ROWS, D), F32),
             pltpu.VMEM((NX * NC, 2, D), F32),
             pltpu.VMEM((NY * NH, 2, D), F32),
-            pltpu.VMEM((ROWS, HALF * 2 + EXTRA), BF16),
-            pltpu.VMEM((NX, NH, NC, ROWS, HALF + EXTRA), BF16),
+            pltpu.VMEM((ROWS, HALF * 2), BF16),
+            pltpu.VMEM((NX, NH, NC, ROWS, HALF), BF16),
+            pltpu.VMEM((OVER, 128), BF16),
+            pltpu.VMEM((NX, NH, NC, OVER, 128), BF16),
+            pltpu.VMEM((OVER, NH * NC * ROWS), F32),
             dma((3,)), dma,
             dma((3, 2)), dma((4, 2)), dma((4, 2)), dma((4, 2)), dma((1,)), dma((1,)),
             dma((3, UNITS + 1)), dma((3, UNITS + 1)), dma((UNITS + 1,)), dma((UNITS + 1,)),

time: 121 us -> 118 us (0.975)
  Pallas kernels: 120 us -> 116 us
    pallas_call x1, Pallas kernels: 117 us -> 113 us  [local(): pl.pallas_call(kernel, out_shape=(pltpu.VMEM((D, NC * SLOTS * ROWS), BF16...]
where the time goes in v5:
time: 118 us; the launch traced here: 117 us
  Pallas kernels  116 us (98%)
    pallas_call x1, Pallas kernels, local(): pl.pallas_call(kernel, out_shape=(pltpu.VMEM((D, NC * SLOTS * ROWS), BF16...  113 us
    pallas_call x1, Pallas kernels, local(): pl.pallas_call(write, out_shape=[pltpu.HBM(r.shape, r.dtype) for r in res...  3.3 us

profile of v5, /device:TPU:1, one launch (start us, length us, event | category | flops | bytes accessed | tf_op | source)
XLA Modules:
  0.0 117.1 jit_solution(8303302485356842483)
XLA Ops:
  0.6 113.1 %factored_step.1 = (bf16[2080,1536]{1,0:T(8,128)(2,1)S(1)}, f32[96,2080]{1,0:T(8,128)S(1)}, f32[96,2080]{1,0:T(8,128)S(1)}, f32[1,96]{1,0:T(1,128)S(1)}, f32[1,2080]{1,0:T(1,128)S(1)}) custom-call(bf16[512,1536]{1,0:T(8,128)(2,1)} %bitcast.11, bf16[520,512]{1,0:T(8,128)(2,1)} %bitcast.15, f32[96,2080]{1,0:T(8,128)} %bitcast.12, f32[1,96]{1,0:T(1,128)} %row_ref.1, ...), custom_call_target="tpu_custom_call" | custom-call | flops 3271557120 | bytes 16777216 | tf_op jit(solution)/shard_map/factored_step/pallas_call | solution.py:559
  113.8 3.3 %write_results.1 = (bf16[2080,1536]{1,0:T(8,128)(2,1)}, f32[96,2080]{1,0:T(8,128)}, f32[96,2080]{1,0:T(8,128)}, f32[1,96]{1,0:T(1,128)}, f32[1,2080]{1,0:T(1,128)}) custom-call(bf16[2080,1536]{1,0:T(8,128)(2,1)S(1)} %get-tuple-element.15.refs_0_, f32[96,2080]{1,0:T(8,128)S(1)} %get-tuple-element.16.refs_1_, f32[96,2080]{1,0:T(8,128)S(1)} %get-tuple-element.17.refs_2_, ...), custom_call_target="tpu_custom_call" | custom-call | tf_op jit(solution)/shard_map/write_results/pallas_call | solution.py:610

commit v6 on v5

--- a/solution.py
+++ b/solution.py
@@ -87,7 +87,7 @@
     return [w + last_place(w) * (q * (1.0 / 1024)) for w, q in zip(wides, shifted)]
 
 
-GX, GZ = 3, 2
+GX, GZ = 3, 3
 HALVES = (pl.ds(0, UNIT), pl.ds(UNIT, HELD - UNIT))
 PAIR = NH * ROWS
 

time: 118 us -> 118 us (level); the launches traced: 117 us -> 118 us
  Pallas kernels: 116 us -> 118 us
    pallas_call x1, Pallas kernels: 113 us -> 114 us  [local(): pl.pallas_call(kernel, out_shape=(pltpu.VMEM((D, NC * SLOTS * ROWS), BF16...]
where the time goes in v6:
time: 118 us
  Pallas kernels  118 us (100%)
    pallas_call x1, Pallas kernels, local(): pl.pallas_call(kernel, out_shape=(pltpu.VMEM((D, NC * SLOTS * ROWS), BF16...  114 us
    pallas_call x1, Pallas kernels, local(): pl.pallas_call(write, out_shape=[pltpu.HBM(r.shape, r.dtype) for r in res...  3.3 us

profile of v6, /device:TPU:1, one launch (start us, length us, event | category | flops | bytes accessed | tf_op | source)
XLA Modules:
  0.0 118.3 jit_solution(14206778950585032670)
XLA Ops:
  0.6 114.4 %factored_step.1 = (bf16[2080,1536]{1,0:T(8,128)(2,1)S(1)}, f32[96,2080]{1,0:T(8,128)S(1)}, f32[96,2080]{1,0:T(8,128)S(1)}, f32[1,96]{1,0:T(1,128)S(1)}, f32[1,2080]{1,0:T(1,128)S(1)}) custom-call(bf16[512,1536]{1,0:T(8,128)(2,1)} %bitcast.11, bf16[520,512]{1,0:T(8,128)(2,1)} %bitcast.15, f32[96,2080]{1,0:T(8,128)} %bitcast.12, f32[1,96]{1,0:T(1,128)} %row_ref.1, ...), custom_call_target="tpu_custom_call" | custom-call | flops 3271557120 | bytes 16777216 | tf_op jit(solution)/shard_map/factored_step/pallas_call | solution.py:559
  115.0 3.3 %write_results.1 = (bf16[2080,1536]{1,0:T(8,128)(2,1)}, f32[96,2080]{1,0:T(8,128)}, f32[96,2080]{1,0:T(8,128)}, f32[1,96]{1,0:T(1,128)}, f32[1,2080]{1,0:T(1,128)}) custom-call(bf16[2080,1536]{1,0:T(8,128)(2,1)S(1)} %get-tuple-element.15.refs_0_, f32[96,2080]{1,0:T(8,128)S(1)} %get-tuple-element.16.refs_1_, f32[96,2080]{1,0:T(8,128)S(1)} %get-tuple-element.17.refs_2_, ...), custom_call_target="tpu_custom_call" | custom-call | tf_op jit(solution)/shard_map/write_results/pallas_call | solution.py:610
